TPU v7x, 256 devices: a whole 4x4x8 slice. The times are simulated.
256 devices in a mesh: section: 2 (over core), ctx: 16 (over z, y_lo), tp: 8 (over y_hi, x).
Axes of the slice: x: 4, y: 4 (y_hi: 2, y_lo: 2; y = y_hi * 2 + y_lo), z: 8, core: 2. Of those that a mesh axis runs over, the one named last changes fastest.
Arguments:
- layer_input: bfloat16 [2, 1, 2048, 4096], P('section', None, 'ctx', 'tp'), may hold values from -6 to 6
- loss_cot: bfloat16 [1, 2048, 4096], P(None, 'ctx', 'tp'), may hold values from -6 to 6
- token_weights: int32 [1, 2048], P(None, 'ctx'), may hold values from 0 to 3
- doc_blocks: int32 [1, 3], replicated, may hold values from 1 to 10, 16 in all within a row
- norm_gain: float32 [2, 4096], P('section'), may hold values from 0.5 to 1.5
- qkv_weight: bfloat16 [2, 4096, 6144], P('section', None, 'tp'), may hold values from -12 to 12, as said below
- out_weight: bfloat16 [2, 4096, 4096], P('section', None, 'tp'), may hold values from -0.09375 to 0.09375
Outputs:
- grad_inputs: bfloat16 [2, 1, 2048, 4096], P('section', None, 'ctx', 'tp')
- grad_qkv: float32 [2, 4096, 6144], P('section', 'ctx', 'tp')
- grad_out: float32 [2, 4096, 4096], P('section', 'ctx', 'tp')
Inputs may be any that keep to these rules, and one draw needn't show every extreme that they name: `doc_blocks`: each row sums to 16, and its longest document has the max. `qkv_weight`: entries of order 4096 ** -0.5 in the query and value columns.
All inputs are finite; a program needn't handle non-finite values.
Results may differ from a plain program's by a relative error of at most 0.04.
The roundings to bfloat16 on the way count: a program that leaves them out, or rounds other values in their place, can miss the bound.
Values may be sent and summed in bfloat16 or wider, within the bound.
A program may use at most 128 MiB of HBM per device.

v0:
```python
import jax
import jax.numpy as jnp
from jax import lax
from jax.sharding import PartitionSpec as P

QUERY_HEADS = 32
KEY_VALUE_HEADS = 8
HEAD_SIZE = 128
BLOCK = 128


EPSILON = 1e-05
NEG_FILL = -1e30


def passed_along(block, axis, distance):
    devices = range(lax.axis_size(axis))
    route = [(i - distance, i) for i in devices if i - distance in devices]
    return lax.ppermute(block, axis, route)


def segment_of(blocks, positions):
    doc_ends = jnp.cumsum(blocks) * BLOCK
    return jnp.sum((positions[:, None] >= doc_ends[None, :]).astype(jnp.int32), axis=1)


def body(layer_input, loss_cot, token_weights, doc_blocks, norm_gain, qkv_weight, out_weight):
    section_count = lax.axis_size("section")
    ctx_count = lax.axis_size("ctx")
    tp_count = lax.axis_size("tp")
    section_pos = lax.axis_index("section")
    ctx_pos = lax.axis_index("ctx")
    tp_pos = lax.axis_index("tp")
    micro_count = layer_input.shape[1]
    number_rows = layer_input.shape[2]
    part_width = layer_input.shape[3]
    full_width = part_width * tp_count
    seq_len = number_rows * ctx_count
    heads_per_group = QUERY_HEADS // KEY_VALUE_HEADS
    joined_cols = qkv_weight.shape[2]
    head_cols = out_weight.shape[2]
    local_groups = joined_cols // ((heads_per_group + 2) * HEAD_SIZE)
    gain_full = norm_gain[0]
    joined_weight = qkv_weight[0]
    output_weight = out_weight[0]
    score_scale = HEAD_SIZE ** (-0.5)
    key_pos = jnp.arange(seq_len, dtype=jnp.int32)
    query_pos = ctx_pos * number_rows + jnp.arange(number_rows, dtype=jnp.int32)
    is_last = section_pos == section_count - 1
    received = jnp.zeros((number_rows, part_width), jnp.bfloat16)
    grads_in = jnp.zeros((micro_count, number_rows, part_width), jnp.bfloat16)
    hidden_store = jnp.zeros((micro_count, number_rows, full_width), jnp.bfloat16)
    joined_store = jnp.zeros((micro_count, number_rows, joined_cols), jnp.bfloat16)
    cot_store = jnp.zeros((micro_count, number_rows, full_width), jnp.bfloat16)
    attended_store = jnp.zeros((micro_count, number_rows, head_cols), jnp.bfloat16)
    step_count = micro_count + section_count - 1
    for step_index in range(step_count):
        micro_index = step_index - (section_count - 1 - section_pos)
        is_valid = (micro_index >= 0) & (micro_index < micro_count)
        chosen = jnp.clip(micro_index, 0, micro_count - 1)
        rows_in = lax.dynamic_index_in_dim(layer_input[0], chosen, 0, keepdims=False)
        loss_rows = lax.dynamic_index_in_dim(loss_cot, chosen, 0, keepdims=False)
        weight_rows = lax.dynamic_index_in_dim(token_weights, chosen, 0, keepdims=False)
        from_loss = (
            loss_rows.astype(jnp.float32) * weight_rows.astype(jnp.float32)[:, None]
        ).astype(jnp.bfloat16)
        cot_local = jnp.where(is_last, from_loss, received)
        rows_full, cot_full = (
            lax.all_gather(rows_in, "tp", axis=1, tiled=True),
            lax.all_gather(cot_local, "tp", axis=1, tiled=True),
        )
        widened = rows_full.astype(jnp.float32)
        inv_rms = lax.rsqrt(jnp.mean(widened * widened, axis=-1, keepdims=True) + EPSILON)
        normed = widened * inv_rms
        hidden = (normed * gain_full).astype(jnp.bfloat16)
        combined_rows = jnp.dot(hidden, joined_weight, preferred_element_type=jnp.float32).astype(
            jnp.bfloat16
        )
        combined_rows = combined_rows.reshape(
            number_rows, local_groups, heads_per_group + 2, HEAD_SIZE
        )
        queries = combined_rows[:, :, :heads_per_group]
        key_value = combined_rows[:, :, heads_per_group:].reshape(
            number_rows, local_groups * 2 * HEAD_SIZE
        )
        key_value_all = lax.all_gather(key_value, "ctx", axis=0, tiled=True).reshape(
            seq_len, local_groups, 2, HEAD_SIZE
        )
        keys_all = key_value_all[:, :, 0]
        values_all = key_value_all[:, :, 1]
        head_cotangent = jnp.dot(
            cot_full, output_weight, preferred_element_type=jnp.float32
        ).astype(jnp.bfloat16)
        head_cotangent = head_cotangent.reshape(
            number_rows, local_groups, heads_per_group, HEAD_SIZE
        )
        blocks = lax.dynamic_index_in_dim(doc_blocks, chosen, 0, keepdims=False)
        segments = segment_of(blocks, key_pos)
        query_seg = lax.dynamic_slice_in_dim(segments, ctx_pos * number_rows, number_rows, 0)
        allowed = (key_pos[None, :] <= query_pos[:, None]) & (
            segments[None, :] == query_seg[:, None]
        )
        scores = (
            jnp.einsum("rgjd,sgd->gjrs", queries, keys_all, preferred_element_type=jnp.float32)
            * score_scale
        )
        scores = jnp.where(allowed[None, None], scores, NEG_FILL)
        row_peak = jnp.max(scores, axis=-1, keepdims=True)
        shifted_exp = jnp.exp(scores - row_peak)
        soft_weights = shifted_exp / jnp.sum(shifted_exp, axis=-1, keepdims=True)
        soft_low = soft_weights.astype(jnp.bfloat16)
        attended = jnp.einsum(
            "gjrs,sgd->rgjd", soft_low, values_all, preferred_element_type=jnp.float32
        ).astype(jnp.bfloat16)
        delta_rows = jnp.einsum(
            "rgjd,rgjd->gjr", head_cotangent, attended, preferred_element_type=jnp.float32
        )
        dprobs = jnp.einsum(
            "rgjd,sgd->gjrs", head_cotangent, values_all, preferred_element_type=jnp.float32
        )
        dscores = (soft_weights * (dprobs - delta_rows[..., None])).astype(jnp.bfloat16)
        query_gradient = (
            jnp.einsum("gjrs,sgd->rgjd", dscores, keys_all, preferred_element_type=jnp.float32)
            * score_scale
        ).astype(jnp.bfloat16)
        grad_keys = (
            jnp.einsum("gjrs,rgjd->sgd", dscores, queries, preferred_element_type=jnp.float32)
            * score_scale
        )
        grad_values = jnp.einsum(
            "gjrs,rgjd->sgd", soft_low, head_cotangent, preferred_element_type=jnp.float32
        )
        key_terms = jnp.stack([grad_keys, grad_values], axis=2).reshape(
            seq_len, local_groups * 2 * HEAD_SIZE
        )
        key_sums = lax.psum_scatter(
            key_terms.astype(jnp.bfloat16), "ctx", scatter_dimension=0, tiled=True
        )
        key_sums = key_sums.reshape(number_rows, local_groups, 2, HEAD_SIZE)
        combined_gradient = jnp.concatenate([query_gradient, key_sums], axis=2).reshape(
            number_rows, joined_cols
        )
        feature_part = lax.dot_general(
            combined_gradient,
            joined_weight,
            (((1,), (1,)), ((), ())),
            preferred_element_type=jnp.float32,
        )
        feature_grad = lax.psum(feature_part.astype(jnp.bfloat16), "tp").astype(jnp.float32)
        scaled = feature_grad * gain_full
        mean_term = jnp.mean(scaled * normed, axis=-1, keepdims=True)
        full_grad = inv_rms * (scaled - normed * mean_term)
        norm_grad = lax.dynamic_slice_in_dim(full_grad, tp_pos * part_width, part_width, 1)
        input_grad = (cot_local.astype(jnp.float32) + norm_grad).astype(jnp.bfloat16)
        grads_in = jnp.where(
            is_valid, lax.dynamic_update_index_in_dim(grads_in, input_grad, chosen, 0), grads_in
        )
        hidden_store = jnp.where(
            is_valid, lax.dynamic_update_index_in_dim(hidden_store, hidden, chosen, 0), hidden_store
        )
        joined_store = jnp.where(
            is_valid,
            lax.dynamic_update_index_in_dim(joined_store, combined_gradient, chosen, 0),
            joined_store,
        )
        cot_store = jnp.where(
            is_valid, lax.dynamic_update_index_in_dim(cot_store, cot_full, chosen, 0), cot_store
        )
        attended_flat = attended.reshape(number_rows, head_cols)
        attended_store = jnp.where(
            is_valid,
            lax.dynamic_update_index_in_dim(attended_store, attended_flat, chosen, 0),
            attended_store,
        )
        if step_index + 1 < step_count:
            received = passed_along(input_grad, "section", -1)
    all_rows = micro_count * number_rows
    hidden_flat = hidden_store.reshape(all_rows, full_width)
    cot_flat = cot_store.reshape(all_rows, full_width)
    joined_flat = joined_store.reshape(all_rows, joined_cols)
    attended_all = attended_store.reshape(all_rows, head_cols)
    upper_block = jnp.concatenate(
        [joined_flat, jnp.zeros((all_rows, head_cols), jnp.bfloat16)], axis=1
    )
    lower_block = jnp.concatenate(
        [jnp.zeros((all_rows, joined_cols), jnp.bfloat16), attended_all], axis=1
    )
    right_blocks = jnp.concatenate([upper_block, lower_block], axis=0)
    left_rows = jnp.concatenate([hidden_flat, cot_flat], axis=0)
    summed = lax.psum_scatter(
        lax.dot_general(
            left_rows, right_blocks, (((0,), (0,)), ((), ())), preferred_element_type=jnp.float32
        ).astype(jnp.bfloat16),
        "ctx",
        scatter_dimension=0,
        tiled=True,
    ).astype(jnp.float32)
    return (grads_in[None], summed[:, :joined_cols][None], summed[:, joined_cols:][None])


def solution(mesh):
    placed = (
        P("section", None, "ctx", "tp"),
        P(None, "ctx", "tp"),
        P(None, "ctx"),
        P(),
        P("section", None),
        P("section", None, "tp"),
        P("section", None, "tp"),
    )
    return jax.shard_map(
        body,
        mesh=mesh,
        in_specs=placed,
        out_specs=(
            P("section", None, "ctx", "tp"),
            P("section", "ctx", "tp"),
            P("section", "ctx", "tp"),
        ),
        check_vma=False,
    )
```

profile of v0, /device:TPU:2, one launch (start us, length us, event | category | flops | bytes accessed | tf_op | source)
XLA Modules:
  0.0 850.4 jit_solution(9138187706730931374)
XLA Ops:
  10.8 55.6 %all-gather.12.cloned.1.call-done = bf16[1,1,128,4096]{3,2,1,0:T(8,128)(2,1)} async-done(((bf16[1,1,128,512]{3,2,1,0:T(8,128)(2,1)}), bf16[1,1,128,4096]{3,2,1,0:T(8,128)(2,1)}) %all-gather.12.cloned.1.call-update) | async-done | bytes 1048592 | tf_op jit(solution)/shard_map/all_gather | solution.py:69
  68.5 4.2 fusion.44
  74.3 47.4 %all-gather.8.cloned.1.call-done = bf16[128,4096]{1,0:T(8,128)(2,1)} async-done(((bf16[128,512]{1,0:T(8,128)(2,1)}), bf16[128,4096]{1,0:T(8,128)(2,1)}) %all-gather.8.cloned.1.call-update) | async-done | bytes 1048592 | tf_op jit(solution)/shard_map/all_gather | solution.py:70
  121.7 3.2 fusion.52
  125.3 66.1 %all-gather.6.cloned.1.call-done = bf16[2048,256]{0,1:T(8,128)(2,1)} async-done(((bf16[128,256]{0,1:T(8,128)(2,1)}), bf16[2048,256]{0,1:T(8,128)(2,1)}) %all-gather.6.cloned.1.call-update) | async-done | bytes 1048592 | tf_op jit(solution)/shard_map/all_gather | solution.py:86
  191.4 1.8 fusion.88
  202.5 69.3 %reduce-scatter.10.cloned.1.call-done = bf16[128,256]{1,0:T(8,128)(2,1)} async-done(((bf16[2048,256]{1,0:T(8,128)(2,1)}), bf16[128,256]{1,0:T(8,128)(2,1)}) %reduce-scatter.10.cloned.1.call-update) | async-done | bytes 65552
  272.8 6.1 fusion.6
  279.0 87.7 %all-reduce.5.cloned.1.call-done = bf16[128,4096]{1,0:T(8,128)(2,1)} async-done(((bf16[128,4096]{1,0:T(8,128)(2,1)}), bf16[128,4096]{1,0:T(8,128)(2,1)}) %all-reduce.5.cloned.1.call-update) | async-done | bytes 1048592 | tf_op jit(solution)/shard_map/psum | solution.py:149
  366.7 1.8 multiply_reduce_fusion.1
  371.3 1.9 collective-permute-done
  374.3 54.4 %all-gather.10.cloned.1.call-done = bf16[128,4096]{1,0:T(8,128)(2,1)} async-done(((bf16[128,512]{1,0:T(8,128)(2,1)}), bf16[128,4096]{1,0:T(8,128)(2,1)}) %all-gather.10.cloned.1.call-update) | async-done | bytes 1048592 | tf_op jit(solution)/shard_map/all_gather | solution.py:70
  428.7 3.2 fusion.55
  432.8 3.9 fusion.30
  436.9 3.7 fusion.23
  442.6 2.3 copy.132
  448.9 2.1 fusion.58
  451.0 64.9 %reduce-scatter.12.cloned.1.call-done = bf16[128,256]{1,0:T(8,128)(2,1)} async-done(((bf16[2048,256]{1,0:T(8,128)(2,1)}), bf16[128,256]{1,0:T(8,128)(2,1)}) %reduce-scatter.12.cloned.1.call-update) | async-done | bytes 65552
  517.8 6.1 fusion.9
  525.3 8.5 convolution_convert_fusion
  533.8 78.1 %all-reduce.7.cloned.1.call-done = bf16[128,4096]{1,0:T(8,128)(2,1)} async-done(((bf16[128,4096]{1,0:T(8,128)(2,1)}), bf16[128,4096]{1,0:T(8,128)(2,1)}) %all-reduce.7.cloned.1.call-update) | async-done | bytes 1048592 | tf_op jit(solution)/shard_map/psum | solution.py:149
  611.9 1.8 multiply_reduce_fusion
  613.7 1.8 fusion.78
  615.4 225.4 %reduce-scatter.8.cloned.1.call-done = bf16[256,1280]{1,0:T(8,128)(2,1)} async-done(((bf16[4096,1280]{1,0:T(8,128)(2,1)}), bf16[256,1280]{1,0:T(8,128)(2,1)}) %reduce-scatter.8.cloned.1.call-update) | async-done | bytes 655376 | tf_op jit(solution)/shard_map/reduce_scatter | solution.py:190
  (120 shorter events, 34.8 us)
Async XLA Ops:
  7.2 59.3 %all-gather.12.cloned.1.call-start = ((), (), s32[]{:S(2)}) async-start(), calls=%async_computation.9 | async-start | bytes 1179648 | tf_op jit(solution)/shard_map/all_gather | solution.py:69
  7.9 113.8 %all-gather.8.cloned.1.call-start = ((), (), s32[]{:S(2)}) async-start(), calls=%async_computation.4 | async-start | bytes 1179648 | tf_op jit(solution)/shard_map/all_gather | solution.py:70
  10.8 180.6 %all-gather.6.cloned.1.call-start = ((), (), s32[]{:S(2)}) async-start(), calls=%async_computation.3 | async-start | bytes 1114112 | tf_op jit(solution)/shard_map/all_gather | solution.py:86
  67.9 5.6 copy-start.25
  73.5 198.3 %reduce-scatter.10.cloned.1.call-start = ((), (), s32[]{:S(2)}) async-start(), calls=%async_computation.10 | async-start | bytes 1114112
  201.0 165.8 %all-reduce.5.cloned.1.call-start = ((), (), s32[]{:S(2)}) async-start(), calls=%async_computation.5 | async-start | bytes 2097152 | tf_op jit(solution)/shard_map/psum | solution.py:149
  272.8 93.9 %copy-start = (bf16[1,1,128,4096]{3,2,1,0:T(8,128)(2,1)S(1)}, bf16[1,1,128,4096]{3,2,1,0:T(8,128)(2,1)}, u32[]{:S(2)}) copy-start(bf16[1,1,128,4096]{3,2,1,0:T(8,128)(2,1)} %all-gather.12.cloned.1.call-done) | copy-start | bytes 3145732
  272.8 93.9 %copy-start.13 = (f32[1,4096]{1,0:T(1,128)S(1)}, f32[1,4096]{1,0:T(1,128)}, u32[]{:S(2)}) copy-start(f32[1,4096]{1,0:T(1,128)} %param.11) | copy-start | bytes 49156
  272.8 93.9 %copy-start.16 = (f32[128]{0:T(128)S(1)}, f32[128]{0:T(128)}, u32[]{:S(2)}) copy-start(f32[128]{0:T(128)} %copy-done.15) | copy-start | bytes 1540
  278.9 90.9 %copy-start.6 = (bf16[1,128,512]{2,1,0:T(8,128)(2,1)S(1)}, bf16[1,128,512]{2,1,0:T(8,128)(2,1)}, u32[]{:S(2)}) copy-start(bf16[1,128,512]{2,1,0:T(8,128)(2,1)} %param.8) | copy-start | bytes 393220
  278.9 90.9 %copy-start.20 = (f32[128]{0:T(128)S(1)}, f32[128]{0:T(128)}, u32[]{:S(2)}) copy-start(f32[128]{0:T(128)} %copy-done.19) | copy-start | bytes 1540
  279.0 149.7 %all-gather.10.cloned.1.call-start = ((), (), s32[]{:S(2)}) async-start(), calls=%async_computation.6 | async-start | bytes 1179648 | tf_op jit(solution)/shard_map/all_gather | solution.py:70
  368.5 64.3 %copy-start.22 = (f32[4,128]{1,0:T(4,128)S(1)}, f32[4,128]{1,0:T(4,128)}, u32[]{:S(2)}) copy-start(f32[4,128]{1,0:T(4,128)} %copy-done.21) | copy-start | bytes 6148
  368.5 64.3 %copy-start.24 = (f32[4,128]{1,0:T(4,128)S(1)}, f32[4,128]{1,0:T(4,128)}, u32[]{:S(2)}) copy-start(f32[4,128]{1,0:T(4,128)} %copy-done.23) | copy-start | bytes 6148
  370.0 62.0 %copy-start.10 = (bf16[128,512]{1,0:T(8,128)(2,1)}, bf16[128,512]{1,0:T(8,128)(2,1)S(1)}, u32[]{:S(2)}) copy-start(bf16[128,512]{1,0:T(8,128)(2,1)S(1)} %fusion.75) | copy-start | bytes 393220
  370.0 3.2 collective-permute-start
  374.0 141.9 %reduce-scatter.12.cloned.1.call-start = ((), (), s32[]{:S(2)}) async-start(), calls=%async_computation.11 | async-start | bytes 1114112
  444.9 167.0 %all-reduce.7.cloned.1.call-start = ((), (), s32[]{:S(2)}) async-start(), calls=%async_computation.7 | async-start | bytes 2097152 | tf_op jit(solution)/shard_map/psum | solution.py:149
  517.8 6.2 copy-start.2
  517.8 6.2 copy-start.3
  523.9 317.0 %reduce-scatter.8.cloned.1.call-start = ((), (), s32[]{:S(2)}) async-start(), calls=%async_computation.8 | async-start | bytes 11141120 | tf_op jit(solution)/shard_map/reduce_scatter | solution.py:190
  533.7 78.2 %copy-start.18 = (f32[128]{0:T(128)S(1)}, f32[128]{0:T(128)}, u32[]{:S(2)}) copy-start(f32[128]{0:T(128)} %copy-done.15) | copy-start | bytes 1540
  533.8 79.9 %copy-start.5 = (bf16[128,512]{1,0:T(8,128)(2,1)S(1)}, bf16[128,512]{1,0:T(8,128)(2,1)}, u32[]{:S(2)}) copy-start(bf16[128,512]{1,0:T(8,128)(2,1)} %broadcast_select_fusion) | copy-start | bytes 393220
  533.8 79.9 %copy-start.11 = (bf16[128,512]{1,0:T(8,128)(2,1)S(1)}, bf16[128,512]{1,0:T(8,128)(2,1)}, u32[]{:S(2)}) copy-start(bf16[128,512]{1,0:T(8,128)(2,1)} %copy-done.10) | copy-start | bytes 393220
  (12 other events, 34.0 us)
Sparse Core Ops, SparseCore 0:
  10.5 55.9 all-gather.11
  69.5 52.1 all-gather.7
  123.9 67.3 all-gather.5
  201.1 70.6 reduce-scatter.9
  279.1 87.5 all-reduce.4
  374.2 54.4 all-gather.9
  445.0 70.8 reduce-scatter.11
  524.0 87.8 all-reduce.6
  614.5 226.3 reduce-scatter.7
where the time goes:
time: 852 us; the launch traced here: 850 us
  waiting for transfers between devices  752 us (88%)
  matrix products  49.7 us (6%)
  other arithmetic  18.8 us (2%)
  between operations  14.3 us (2%)
  local copies, waits for them, and re-layouts  14 us (2%)
    reduce_scatter x1, waiting for transfers between devices, body(): lax.psum_scatter(lax.dot_general(left_rows, right_blocks, (((0,), (0,)),...  225 us
    psum x2, waiting for transfers between devices, body(): lax.psum(feature_part.astype(jnp.bfloat16), 'tp').astype(jnp.float32)  166 us
    unnamed x11, waiting for transfers between devices  135 us
    all_gather x2, waiting for transfers between devices, body(): lax.all_gather(cot_local, 'tp', axis=1, tiled=True)  102 us
    all_gather x1, waiting for transfers between devices, body(): lax.all_gather(key_value, 'ctx', axis=0, tiled=True)  66.1 us
    all_gather x1, waiting for transfers between devices, body(): lax.all_gather(rows_in, 'tp', axis=1, tiled=True)  55.6 us
  transfers between devices with their start and end apart: 10, of which 10 were waited for; matrix products, arithmetic and copies ran while one was open for 4% of the time, Pallas kernels for 0%

commit v1 on v0

v1 whole, which is shorter than its diff:
```python
import functools

import jax
import jax.numpy as jnp
from jax import lax
from jax.experimental import pallas as pl
from jax.experimental.pallas import tpu as pltpu
from jax.sharding import PartitionSpec as P

MESH = pl.DeviceIdType.MESH
GROUP_HEADS = 4
HEAD_SIZE = 128
BLOCK = 128
MAX_DOC = 10
EPSILON = 1e-05
NEG_FILL = -1e30
F32 = jnp.float32
BF16 = jnp.bfloat16

NN = (((1,), (0,)), ((), ()))
NT = (((1,), (1,)), ((), ()))
TN = (((0,), (0,)), ((), ()))


def mm(a, b, dims=NN):
    return lax.dot_general(a, b, dims, preferred_element_type=F32)


def kernel(
    n_ctx, n_tp, window,
    x_ref, loss_ref, tw_ref, docs_ref, gain_ref, wq_hbm, wo_hbm,
    gin_ref, gqkv_ref, gout_ref,
    wq, wo, xfull, cotfull, cot_loc, inv_b,
    kv, q_s, hc_s, att_s, att_n, gq_n, gkv_n, scores, probs, peak, denom, acc,
    dkv_part, dkv_in, feat_f, feat_out, feat_in, rs_out, rs_in,
    hid_z, cot_z, att_z, gq_z, gkv_z, y_out_o, y_out_q, y_out_k, y_in_o, y_in_q, y_in_k,
    w_sem, x_s, x_r, c_s, c_r, kv_s, kv_r, d_s, d_r, f_s, f_r, r_s, r_r,
    hz_s, hz_r, cz_s, cz_r, az_s, az_r, qz_s, qz_r, kz_s, kz_r, y_s, y_r, sec_s, sec_r,
):
    s = lax.axis_index("section")
    c = lax.axis_index("ctx")
    t = lax.axis_index("tp")
    n_z = n_ctx // 2
    z, lo = c // 2, lax.rem(c, 2)
    part = x_ref.shape[1]
    width = part * n_tp
    half = part // 2
    heads = GROUP_HEADS * HEAD_SIZE
    cols = heads + 2 * HEAD_SIZE
    scale = HEAD_SIZE ** (-0.5)
    last = window - 1

    def remote(src, dst, ss, rs, dev):
        return pltpu.make_async_remote_copy(
            src_ref=src, dst_ref=dst, send_sem=ss, recv_sem=rs, device_id=dev, device_id_type=MESH
        )

    def tp_dev(p):
        return {"tp": p}

    def z_dev(p):
        return {"ctx": p * 2 + lo}

    def exchange(n, me, dev, src_of, slot, ss, rs):
        def copy_to(p):
            return remote(src_of(p), slot(me), ss.at[p], rs.at[me], dev(p))

        def copy_from(p):
            return remote(slot(p), slot(p), ss.at[p], rs.at[p], dev(p))

        def start():
            @pl.loop(1, n)
            def _(i):
                copy_to(lax.rem(me + i, n)).start()

        def wait_recv():
            @pl.loop(1, n)
            def _(i):
                copy_from(lax.rem(me + i, n)).wait_recv()

        def wait_send():
            @pl.loop(1, n)
            def _(i):
                copy_to(lax.rem(me + i, n)).wait_send()

        return start, wait_recv, wait_send, copy_to

    rows = lambda ref: lambda p: ref.at[pl.ds(p * BLOCK, BLOCK)]
    whole = lambda ref: lambda p: ref

    x_ex = exchange(n_tp, t, tp_dev, whole(x_ref), lambda p: xfull.at[p], x_s, x_r)
    c_ex = exchange(n_tp, t, tp_dev, whole(cot_loc), lambda p: cotfull.at[p], c_s, c_r)
    f_ex = exchange(n_tp, t, tp_dev, lambda p: feat_out.at[p], lambda p: feat_in.at[p], f_s, f_r)
    r_ex = exchange(n_tp, t, tp_dev, whole(rs_out), lambda p: rs_in.at[p], r_s, r_r)
    hz_ex = exchange(n_z, z, z_dev, lambda p: xfull.at[p], rows(hid_z), hz_s, hz_r)
    cz_ex = exchange(n_z, z, z_dev, lambda p: cotfull.at[p], rows(cot_z), cz_s, cz_r)
    az_ex = exchange(n_z, z, z_dev, whole(att_n), rows(att_z), az_s, az_r)
    qz_ex = exchange(n_z, z, z_dev, whole(gq_n), rows(gq_z), qz_s, qz_r)
    kz_ex = exchange(n_z, z, z_dev, whole(gkv_n), rows(gkv_z), kz_s, kz_r)
    wq_copy = pltpu.make_async_copy(wq_hbm, wq, w_sem.at[0])
    wo_copy = pltpu.make_async_copy(wo_hbm, wo, w_sem.at[1])

    wq_copy.start()
    wo_copy.start()
    kv[...] = jnp.zeros_like(kv)

    barrier = pltpu.get_barrier_semaphore()

    @pl.loop(1, n_tp)
    def _(i):
        pl.semaphore_signal(barrier, inc=1, device_id={"tp": lax.rem(t + i, n_tp)}, device_id_type=MESH)

    @pl.loop(1, n_ctx)
    def _(i):
        pl.semaphore_signal(barrier, inc=1, device_id={"ctx": lax.rem(c + i, n_ctx)}, device_id_type=MESH)

    pl.semaphore_signal(barrier, inc=1, device_id={"section": 1 - s}, device_id_type=MESH)
    pl.semaphore_wait(barrier, n_tp + n_ctx - 1)

    x_ex[0]()
    xfull[t] = x_ref[...]

    @pl.when(s == 1)
    def _():
        weights = jnp.broadcast_to(tw_ref[...].astype(F32), (BLOCK, BLOCK)).T[:, :1]
        cot_loc[...] = (loss_ref[...].astype(F32) * weights).astype(BF16)
        c_ex[0]()

    x_ex[1]()
    square = jnp.zeros((BLOCK, part), F32)
    for p in range(n_tp):
        wide = xfull[p].astype(F32)
        square = square + wide * wide
    inv = lax.rsqrt(jnp.sum(square, axis=1, keepdims=True) / width + EPSILON)
    inv_b[...] = jnp.broadcast_to(inv, inv_b.shape)
    for p in range(n_tp):
        gain = gain_ref[:, p * part : (p + 1) * part]
        xfull[p] = ((xfull[p].astype(F32) * inv) * gain).astype(BF16)

    def project(full, weight, lo_col, n_col):
        total = jnp.zeros((BLOCK, n_col), F32)
        for p in range(n_tp):
            total = total + mm(full[p], weight[p * part : (p + 1) * part, lo_col : lo_col + n_col])
        return total.astype(BF16)

    wq_copy.wait()
    kv[last] = project(xfull, wq, heads, 2 * HEAD_SIZE)

    def kv_copy(d):
        return remote(
            kv.at[last], kv.at[last - d], kv_s.at[d], kv_r.at[d], {"ctx": lax.rem(c + d, n_ctx)}
        )

    @pl.loop(1, window)
    def _(d):
        @pl.when(c + d < n_ctx)
        def _():
            kv_copy(d).start()

    for j in range(0, GROUP_HEADS, 2):
        pair = project(xfull, wq, j * HEAD_SIZE, 2 * HEAD_SIZE)
        q_s[j * BLOCK : (j + 1) * BLOCK] = pair[:, :HEAD_SIZE]
        q_s[(j + 1) * BLOCK : (j + 2) * BLOCK] = pair[:, HEAD_SIZE:]
    hz_ex[0]()
    hid_z[pl.ds(z * BLOCK, BLOCK)] = xfull[z]

    doc_start = jnp.int32(0)
    doc_end = jnp.int32(0)
    for i in range(docs_ref.shape[1]):
        doc_end = doc_end + docs_ref[0, i]
        doc_start = jnp.where(doc_end <= c, doc_end, doc_start)
    own = mm(q_s[...], kv[last, :, :HEAD_SIZE], NT) * scale
    row = lax.broadcasted_iota(jnp.int32, own.shape, 0) % BLOCK
    col = lax.broadcasted_iota(jnp.int32, own.shape, 1)
    own = jnp.where(col <= row, own, NEG_FILL)
    scores[last] = own
    peak[...] = own

    @pl.loop(0, last)
    def _(i):
        j = last - 1 - i

        @pl.when(c - last + j >= 0)
        def _():
            kv_copy(last - j).wait_recv()

        block = mm(q_s[...], kv[j, :, :HEAD_SIZE], NT) * scale
        block = jnp.where(c - last + j >= doc_start, block, NEG_FILL)
        scores[j] = block
        peak[...] = jnp.maximum(peak[...], block)

    peak[...] = jnp.broadcast_to(jnp.max(peak[...], axis=1, keepdims=True), peak.shape)
    denom[...] = jnp.zeros_like(denom)

    @pl.loop(0, window)
    def _(j):
        e = jnp.exp(scores[j] - peak[...])
        scores[j] = e
        denom[...] += e

    denom[...] = jnp.broadcast_to(1.0 / jnp.sum(denom[...], axis=1, keepdims=True), denom.shape)
    acc[...] = jnp.zeros_like(acc)

    @pl.loop(0, window)
    def _(j):
        soft = scores[j] * denom[...]
        low = soft.astype(BF16)
        scores[j] = soft
        probs[j] = low
        acc[...] += mm(low, kv[j, :, HEAD_SIZE:])

    att_s[...] = acc[...].astype(BF16)
    for j in range(GROUP_HEADS):
        att_n[:, j * HEAD_SIZE : (j + 1) * HEAD_SIZE] = att_s[j * BLOCK : (j + 1) * BLOCK]
    az_ex[0]()
    att_z[pl.ds(z * BLOCK, BLOCK)] = att_n[...]

    sec_copy = remote(gin_ref, cot_loc, sec_s, sec_r, {"section": 1 - s})

    @pl.when(s == 0)
    def _():
        sec_copy.wait_recv()
        c_ex[0]()

    cotfull[t] = cot_loc[...]
    wo_copy.wait()
    c_ex[1]()
    for j in range(0, GROUP_HEADS, 2):
        pair = project(cotfull, wo, j * HEAD_SIZE, 2 * HEAD_SIZE)
        hc_s[j * BLOCK : (j + 1) * BLOCK] = pair[:, :HEAD_SIZE]
        hc_s[(j + 1) * BLOCK : (j + 2) * BLOCK] = pair[:, HEAD_SIZE:]

    delta = jnp.sum(hc_s[...].astype(F32) * att_s[...].astype(F32), axis=1, keepdims=True)
    peak[...] = jnp.broadcast_to(delta, peak.shape)
    acc[...] = jnp.zeros_like(acc)

    def dkv_copy(d):
        return remote(
            dkv_part.at[last - d], dkv_in.at[d], d_s.at[d], d_r.at[d],
            {"ctx": lax.rem(c - d + n_ctx, n_ctx)},
        )

    @pl.loop(0, window)
    def _(j):
        dprobs = mm(hc_s[...], kv[j, :, HEAD_SIZE:], NT)
        ds = (scores[j] * (dprobs - peak[...])).astype(BF16)
        acc[...] += mm(ds, kv[j, :, :HEAD_SIZE])
        dkv_part[j, :, :HEAD_SIZE] = (mm(ds, q_s[...], TN) * scale).astype(BF16)
        dkv_part[j, :, HEAD_SIZE:] = mm(probs[j], hc_s[...], TN).astype(BF16)

        @pl.when((j < last) & (c - last + j >= 0))
        def _():
            dkv_copy(last - j).start()

    for j in range(GROUP_HEADS):
        gq_n[:, j * HEAD_SIZE : (j + 1) * HEAD_SIZE] = (
            acc[j * BLOCK : (j + 1) * BLOCK] * scale
        ).astype(BF16)
    qz_ex[0]()
    cz_ex[0]()
    gq_z[pl.ds(z * BLOCK, BLOCK)] = gq_n[...]
    cot_z[pl.ds(z * BLOCK, BLOCK)] = cotfull[z]

    @pl.loop(0, n_tp)
    def _(p):
        feat_f[p] = mm(gq_n[...], wq[pl.ds(p * part, part), :heads], NT)

    acc[:BLOCK] = dkv_part[last, :, :HEAD_SIZE].astype(F32)
    acc[BLOCK : 2 * BLOCK] = dkv_part[last, :, HEAD_SIZE:].astype(F32)

    @pl.loop(1, window)
    def _(d):
        @pl.when(c + d < n_ctx)
        def _():
            dkv_copy(d).wait_recv()
            acc[:BLOCK] += dkv_in[d, :, :HEAD_SIZE].astype(F32)
            acc[BLOCK : 2 * BLOCK] += dkv_in[d, :, HEAD_SIZE:].astype(F32)

    gkv_n[:, :HEAD_SIZE] = acc[:BLOCK].astype(BF16)
    gkv_n[:, HEAD_SIZE:] = acc[BLOCK : 2 * BLOCK].astype(BF16)

    @pl.loop(1, n_tp + 1)
    def _(i):
        p = lax.rem(t + i, n_tp)
        share = feat_f[p] + mm(gkv_n[...], wq[pl.ds(p * part, part), heads:], NT)
        feat_out[p] = share.astype(BF16)

        @pl.when(i < n_tp)
        def _():
            f_ex[3](p).start()

    kz_ex[0]()
    gkv_z[pl.ds(z * BLOCK, BLOCK)] = gkv_n[...]
    feat_in[t] = feat_out[t]
    f_ex[1]()
    feature = jnp.zeros((BLOCK, part), F32)
    for p in range(n_tp):
        feature = feature + feat_in[p].astype(F32)
    inv = inv_b[:, :1]
    gain = gain_ref[:, pl.ds(pl.multiple_of(t * part, part), part)]
    scaled = feature * gain
    normed = x_ref[...].astype(F32) * inv
    row_sum = jnp.sum(scaled * normed, axis=1, keepdims=True)
    rs_out[...] = jnp.broadcast_to(row_sum, (BLOCK, BLOCK)).T[:8]
    r_ex[0]()
    rs_in[t] = rs_out[...]
    r_ex[1]()
    total = rs_in[0]
    for p in range(1, n_tp):
        total = total + rs_in[p]
    mean = jnp.broadcast_to(total[:1] / width, (BLOCK, BLOCK)).T[:, :1]
    gin_ref[...] = (cot_loc[...].astype(F32) + inv * (scaled - normed * mean)).astype(BF16)

    @pl.when(s == 1)
    def _():
        sec_copy.start()

    hz_ex[1]()
    az_ex[1]()
    cz_ex[1]()
    qz_ex[1]()
    kz_ex[1]()
    mate = {"ctx": z * 2 + 1 - lo}
    y_copies = [
        remote(y_out_o, y_in_o, y_s.at[0], y_r.at[0], mate),
        remote(y_out_q, y_in_q, y_s.at[1], y_r.at[1], mate),
        remote(y_out_k, y_in_k, y_s.at[2], y_r.at[2], mate),
    ]
    theirs = pl.ds(pl.multiple_of((1 - lo) * half, half), half)
    mine = pl.ds(pl.multiple_of(lo * half, half), half)
    step = min(256, heads)
    plan = [
        (cot_z, att_z, y_out_o, y_in_o, gout_ref, 0, y_copies[0]),
        (hid_z, gq_z, y_out_q, y_in_q, gqkv_ref, 0, y_copies[1]),
        (hid_z, gkv_z, y_out_k, y_in_k, gqkv_ref, heads, y_copies[2]),
    ]
    for left, right, y_out, _, _, _, copy in plan:
        for k in range(0, right.shape[1], step):
            y_out[:, k : k + step] = mm(left[:, theirs], right[:, k : k + step], TN).astype(BF16)
        copy.start()
    for left, right, _, y_in, out, base, copy in plan:
        for k in range(0, right.shape[1], step):
            out[:, base + k : base + k + step] = mm(left[:, mine], right[:, k : k + step], TN)
        copy.wait_recv()
        for k in range(0, right.shape[1], step):
            out[:, base + k : base + k + step] += y_in[:, k : k + step].astype(F32)

    for ex in (x_ex, c_ex, f_ex, r_ex, hz_ex, cz_ex, az_ex, qz_ex, kz_ex):
        ex[2]()
    for copy in y_copies:
        copy.wait_send()

    @pl.loop(1, window)
    def _(d):
        @pl.when(c + d < n_ctx)
        def _():
            kv_copy(d).wait_send()

        @pl.when(c - d >= 0)
        def _():
            dkv_copy(d).wait_send()

    @pl.when(s == 1)
    def _():
        sec_copy.wait_send()


def body(layer_input, loss_cot, token_weights, doc_blocks, norm_gain, qkv_weight, out_weight):
    n_ctx, n_tp = lax.axis_size("ctx"), lax.axis_size("tp")
    n_z = n_ctx // 2
    part = layer_input.shape[3]
    width = part * n_tp
    cols, heads = qkv_weight.shape[2], out_weight.shape[2]
    window = min(MAX_DOC, n_ctx)
    q_rows = GROUP_HEADS * BLOCK
    kv_cols = 2 * HEAD_SIZE
    half = part // 2
    vmem = lambda shape, dtype=BF16: pltpu.VMEM(shape, dtype)
    dma = lambda *n: pltpu.SemaphoreType.DMA(n)
    scratch = [
        vmem((width, cols)), vmem((width, heads)),
        vmem((n_tp, BLOCK, part)), vmem((n_tp, BLOCK, part)), vmem((BLOCK, part)), vmem((BLOCK, BLOCK), F32),
        vmem((window, BLOCK, kv_cols)),
        vmem((q_rows, HEAD_SIZE)), vmem((q_rows, HEAD_SIZE)), vmem((q_rows, HEAD_SIZE)),
        vmem((BLOCK, heads)), vmem((BLOCK, heads)), vmem((BLOCK, kv_cols)),
        vmem((window, q_rows, BLOCK), F32), vmem((window, q_rows, BLOCK)),
        vmem((q_rows, BLOCK), F32), vmem((q_rows, BLOCK), F32), vmem((q_rows, HEAD_SIZE), F32),
        vmem((window, BLOCK, kv_cols)), vmem((window, BLOCK, kv_cols)),
        vmem((n_tp, BLOCK, part), F32), vmem((n_tp, BLOCK, part)), vmem((n_tp, BLOCK, part)),
        vmem((8, BLOCK), F32), vmem((n_tp, 8, BLOCK), F32),
        vmem((n_z * BLOCK, part)), vmem((n_z * BLOCK, part)), vmem((n_z * BLOCK, heads)),
        vmem((n_z * BLOCK, heads)), vmem((n_z * BLOCK, kv_cols)),
        vmem((half, heads)), vmem((half, heads)), vmem((half, kv_cols)),
        vmem((half, heads)), vmem((half, heads)), vmem((half, kv_cols)),
        dma(2), dma(n_tp), dma(n_tp), dma(n_tp), dma(n_tp), dma(window), dma(window), dma(window), dma(window),
        dma(n_tp), dma(n_tp), dma(n_tp), dma(n_tp),
        dma(n_z), dma(n_z), dma(n_z), dma(n_z), dma(n_z), dma(n_z), dma(n_z), dma(n_z), dma(n_z), dma(n_z),
        dma(3), dma(3), pltpu.SemaphoreType.DMA, pltpu.SemaphoreType.DMA,
    ]
    in_vmem = pl.BlockSpec(memory_space=pltpu.VMEM)
    anywhere = pl.BlockSpec(memory_space=pl.ANY)
    grad_in, grad_qkv, grad_out = pl.pallas_call(
        functools.partial(kernel, n_ctx, n_tp, window),
        out_shape=(
            jax.ShapeDtypeStruct((BLOCK, part), BF16),
            jax.ShapeDtypeStruct((half, cols), F32),
            jax.ShapeDtypeStruct((half, heads), F32),
        ),
        in_specs=[
            in_vmem, in_vmem, in_vmem, pl.BlockSpec(memory_space=pltpu.SMEM), in_vmem, anywhere, anywhere,
        ],
        out_specs=(in_vmem, in_vmem, in_vmem),
        scratch_shapes=scratch,
        compiler_params=pltpu.CompilerParams(
            collective_id=0, has_side_effects=True, vmem_limit_bytes=56 * 1024 * 1024
        ),
    )(
        layer_input[0, 0], loss_cot[0], token_weights, doc_blocks, norm_gain, qkv_weight[0], out_weight[0]
    )
    return grad_in[None, None], grad_qkv[None], grad_out[None]


def solution(mesh):
    placed = (
        P("section", None, "ctx", "tp"),
        P(None, "ctx", "tp"),
        P(None, "ctx"),
        P(),
        P("section", None),
        P("section", None, "tp"),
        P("section", None, "tp"),
    )
    return jax.shard_map(
        body,
        mesh=mesh,
        in_specs=placed,
        out_specs=(
            P("section", None, "ctx", "tp"),
            P("section", "ctx", "tp"),
            P("section", "ctx", "tp"),
        ),
        check_vma=False,
    )
```

time: 852 us -> 176 us (0.21)
  waiting for transfers between devices: 752 us -> 0 us
  Pallas kernels: 0 us -> 167 us
  matrix products: 49.7 us -> 0 us
  other arithmetic: 18.8 us -> 0 us
  between operations: 14.3 us -> 0.64 us
    reduce_scatter x1 -> x0, waiting for transfers between devices: 225 us -> none  [body(): lax.psum_scatter(lax.dot_general(left_rows, right_blocks, (((0,), (0,)),...]
    all_gather x4 -> x0, waiting for transfers between devices: 223 us -> none  [the longest x2 102 us: body(): lax.all_gather(cot_local, 'tp', axis=1, tiled=True)]
    pallas_call x0 -> x1, Pallas kernels: none -> 167 us  [body(): pl.pallas_call(functools.partial(kernel, n_ctx, n_tp, window), out_shape=...]
    psum x2 -> x0, waiting for transfers between devices: 166 us -> none  [body(): lax.psum(feature_part.astype(jnp.bfloat16), 'tp').astype(jnp.float32)]
    unnamed x11 -> x0, waiting for transfers between devices: 135 us -> none
    dot_general x16 -> x0, matrix products: 49.7 us -> none  [the longest x2 12.2 us: body(): lax.dot_general(combined_gradient, joined_weight, (((1,), (1,)), ((), ())...]
  transfers between devices with their start and end apart: 10 -> 0, of which waited for: 10 -> 0; matrix products, arithmetic and copies ran while one was open for 4% -> 0% of each run, Pallas kernels for 0% -> 0%
where the time goes in v1:
time: 176 us; the launch traced here: 174 us
  Pallas kernels  167 us (95%)
  local copies, waits for them, and re-layouts  5.5 us (3%)
    pallas_call x1, Pallas kernels, body(): pl.pallas_call(functools.partial(kernel, n_ctx, n_tp, window), out_shape=...  167 us
    unnamed x3, local copies, waits for them, and re-layouts  5.5 us

profile of v1, /device:TPU:2, one launch (start us, length us, event | category | flops | bytes accessed | tf_op | source)
XLA Modules:
  0.0 173.5 jit_solution(2896641790887614037)
XLA Ops:
  0.6 167.4 %shard_map.94 = (bf16[128,512]{1,0:T(8,128)(2,1)}, f32[256,768]{1,0:T(8,128)}, f32[256,512]{1,0:T(8,128)}) custom-call(bf16[128,512]{1,0:T(8,128)(2,1)} %bitcast.11, bf16[128,512]{1,0:T(8,128)(2,1)} %bitcast.12, s32[1,128]{1,0:T(1,128)} %tw_ref.1, s32[1,3]{1,0:T(1,128)} %docs_ref.1, f32[1,4096]{1,0:T(1,128)} %gain_ref.1, bf16[4096,768]{1,0:T(8,128)(2,1)} %bitcast.7, ...), custom_call_target="tpu_custom_call" | custom-call | tf_op jit(solution)/shard_map/pallas_call | solution.py:402
  168.0 1.6 copy.13
  169.6 2.1 %copy.14 = f32[1,256,768]{2,1,0:T(8,128)} copy(f32[1,256,768]{2,1,0:T(8,128)} %bitcast.9) | data formatting | bytes 1572864
  171.7 1.9 %copy.15 = f32[1,256,512]{2,1,0:T(8,128)} copy(f32[1,256,512]{2,1,0:T(8,128)} %bitcast.10) | data formatting | bytes 1048576

commit v2 on v1

v2 whole, which is shorter than its diff:
```python
import functools

import jax
import jax.numpy as jnp
from jax import lax
from jax.experimental import pallas as pl
from jax.experimental.pallas import tpu as pltpu
from jax.sharding import PartitionSpec as P

MESH = pl.DeviceIdType.MESH
GROUP_HEADS = 4
HEAD_SIZE = 128
BLOCK = 128
MAX_DOC = 10
EPSILON = 1e-05
NEG_FILL = -1e30
F32 = jnp.float32
BF16 = jnp.bfloat16

NN = (((1,), (0,)), ((), ()))
NT = (((1,), (1,)), ((), ()))
TN = (((0,), (0,)), ((), ()))


def mm(a, b, dims=NN):
    return lax.dot_general(a, b, dims, preferred_element_type=F32)


def kernel(
    n_ctx, n_tp, window,
    x_ref, loss_ref, tw_ref, docs_ref, gain_ref, wq_hbm, wo_hbm,
    gin_ref, gqkv_ref, gout_ref,
    wq, wo, xfull, cotfull, cot_loc, inv_b,
    kv, q_s, hc_s, att_s, gq_n, gkv_n, scores, probs, peak, denom, acc,
    dkv_part, dkv_in, feat_f, feat_out, feat_in, rs_out, rs_in,
    hid_p, cot_p, hid_z, cot_z, att_z, gq_z, gkv_z, turned,
    y_out_o, y_out_q, y_out_k, y_in_o, y_in_q, y_in_k,
    w_sem, x_s, x_r, c_s, c_r, kv_s, kv_r, d_s, d_r, f_s, f_r, r_s, r_r,
    h1_s, h1_r, h2_s, h2_r, c1_s, c1_r, c2_s, c2_r, az_s, az_r, qz_s, qz_r, kz_s, kz_r, y_s, y_r, sec_s, sec_r, gate,
):
    s = lax.axis_index("section")
    c = lax.axis_index("ctx")
    t = lax.axis_index("tp")
    n_z = n_ctx // 2
    z, lo = c // 2, lax.rem(c, 2)
    part = x_ref.shape[1]
    width = part * n_tp
    half = part // 2
    heads = GROUP_HEADS * HEAD_SIZE
    cols = heads + 2 * HEAD_SIZE
    scale = HEAD_SIZE ** (-0.5)
    last = window - 1

    def remote(src, dst, ss, rs, dev):
        return pltpu.make_async_remote_copy(
            src_ref=src, dst_ref=dst, send_sem=ss, recv_sem=rs, device_id=dev, device_id_type=MESH
        )

    def tp_dev(p):
        return {"tp": p}

    def z_dev(p):
        return {"ctx": p * 2 + lo}

    def exchange(n, me, dev, src_of, slot, ss, rs):
        def copy_to(p):
            return remote(src_of(p), slot(me), ss.at[p], rs.at[me], dev(p))

        def copy_from(p):
            return remote(slot(p), slot(p), ss.at[p], rs.at[p], dev(p))

        def start():
            @pl.loop(1, n)
            def _(i):
                copy_to(lax.rem(me + i, n)).start()

        def wait_recv():
            @pl.loop(1, n)
            def _(i):
                copy_from(lax.rem(me + i, n)).wait_recv()

        def wait_send():
            @pl.loop(1, n)
            def _(i):
                copy_to(lax.rem(me + i, n)).wait_send()

        return start, wait_recv, wait_send, copy_to

    def ring(ref, ss, rs):
        up, down = z_dev(lax.rem(z + 1, n_z)), z_dev(lax.rem(z + n_z - 1, n_z))
        top = n_z // 2

        def piece(p, k, side):
            if k < top:
                return ref.at[pl.ds(p * BLOCK, BLOCK)]
            return ref.at[pl.ds(p * BLOCK + side * (BLOCK // 2), BLOCK // 2)]

        def pair(k, shift):
            below = piece(lax.rem(z - k + shift + n_z, n_z), k, 0)
            above = piece(lax.rem(z + k - shift, n_z), k, 1)
            return (
                remote(below, below, ss.at[k - 1], rs.at[k - 1], up),
                remote(above, above, ss.at[top + k - 1], rs.at[top + k - 1], down),
            )

        def arrive(k):
            for copy in pair(k, 0):
                copy.wait_recv()

        def stage(k):
            if k > top:
                return
            if k > 1:
                arrive(k - 1)
            for copy in pair(k, 1):
                copy.start()

        def wait_send():
            for k in range(1, top + 1):
                for copy in pair(k, 1):
                    copy.wait_send()

        return stage, lambda: arrive(top), wait_send

    whole = lambda ref: lambda p: ref
    share = BLOCK // n_tp
    my_rows = pl.ds(pl.multiple_of(t * share, share), share)

    x_ex = exchange(n_tp, t, tp_dev, whole(x_ref), lambda p: xfull.at[p], x_s, x_r)
    c_ex = exchange(n_tp, t, tp_dev, whole(cot_loc), lambda p: cotfull.at[p], c_s, c_r)
    f_ex = exchange(n_tp, t, tp_dev, lambda p: feat_out.at[p], lambda p: feat_in.at[p], f_s, f_r)
    r_ex = exchange(n_tp, t, tp_dev, whole(rs_out), lambda p: rs_in.at[p], r_s, r_r)
    h1_ex = exchange(n_z, z, z_dev, lambda p: xfull.at[p, my_rows], lambda p: hid_p.at[p], h1_s, h1_r)
    h2_ex = exchange(n_tp, t, tp_dev, whole(hid_p), lambda p: hid_z.at[:, p], h2_s, h2_r)
    c1_ex = exchange(n_z, z, z_dev, lambda p: cotfull.at[p, my_rows], lambda p: cot_p.at[p], c1_s, c1_r)
    c2_ex = exchange(n_tp, t, tp_dev, whole(cot_p), lambda p: cot_z.at[:, p], c2_s, c2_r)
    att_ring = ring(att_z, az_s, az_r)
    gq_ring = ring(gq_z, qz_s, qz_r)
    gkv_ring = ring(gkv_z, kz_s, kz_r)
    own_z = pl.ds(pl.multiple_of(z * BLOCK, BLOCK), BLOCK)
    wq_copy = pltpu.make_async_copy(wq_hbm, wq, w_sem.at[0])
    wo_copy = pltpu.make_async_copy(wo_hbm, wo, w_sem.at[1])

    wq_copy.start()
    wo_copy.start()
    kv[...] = jnp.zeros_like(kv)

    barrier = pltpu.get_barrier_semaphore()

    @pl.loop(1, n_tp)
    def _(i):
        pl.semaphore_signal(barrier, inc=1, device_id={"tp": lax.rem(t + i, n_tp)}, device_id_type=MESH)

    @pl.loop(1, n_ctx)
    def _(i):
        pl.semaphore_signal(barrier, inc=1, device_id={"ctx": lax.rem(c + i, n_ctx)}, device_id_type=MESH)

    pl.semaphore_signal(barrier, inc=1, device_id={"section": 1 - s}, device_id_type=MESH)
    pl.semaphore_wait(barrier, n_tp + n_ctx - 1)

    @pl.when(s == 0)
    def _():
        pl.semaphore_wait(gate, 1)

    x_ex[0]()
    xfull[t] = x_ref[...]

    @pl.when(s == 1)
    def _():
        weights = jnp.broadcast_to(tw_ref[...].astype(F32), (BLOCK, BLOCK)).T[:, :1]
        cot_loc[...] = (loss_ref[...].astype(F32) * weights).astype(BF16)
        c_ex[0]()

    x_ex[1]()

    @pl.when(s == 1)
    def _():
        pl.semaphore_signal(gate, inc=1, device_id={"section": 1 - s}, device_id_type=MESH)

    square = jnp.zeros((BLOCK, part), F32)
    for p in range(n_tp):
        wide = xfull[p].astype(F32)
        square = square + wide * wide
    inv = lax.rsqrt(jnp.sum(square, axis=1, keepdims=True) / width + EPSILON)
    inv_b[...] = jnp.broadcast_to(inv, inv_b.shape)
    for p in range(n_tp):
        gain = gain_ref[:, p * part : (p + 1) * part]
        xfull[p] = ((xfull[p].astype(F32) * inv) * gain).astype(BF16)

    def project(full, weight, lo_col, n_col):
        total = jnp.zeros((BLOCK, n_col), F32)
        for p in range(n_tp):
            total = total + mm(full[p], weight[p * part : (p + 1) * part, lo_col : lo_col + n_col])
        return total.astype(BF16)

    def slot(j):
        if isinstance(j, int):
            return pl.ds(j * BLOCK, BLOCK)
        return pl.ds(pl.multiple_of(j * BLOCK, BLOCK), BLOCK)

    wq_copy.wait()
    kv[slot(last)] = project(xfull, wq, heads, 2 * HEAD_SIZE)

    def kv_copy(d):
        return remote(
            kv.at[slot(last)], kv.at[slot(last - d)], kv_s.at[d], kv_r.at[d], {"ctx": lax.rem(c + d, n_ctx)}
        )

    @pl.loop(1, window)
    def _(d):
        @pl.when(c + d < n_ctx)
        def _():
            kv_copy(d).start()

    for j in range(0, GROUP_HEADS, 2):
        pair = project(xfull, wq, j * HEAD_SIZE, 2 * HEAD_SIZE)
        q_s[j * BLOCK : (j + 1) * BLOCK] = pair[:, :HEAD_SIZE]
        q_s[(j + 1) * BLOCK : (j + 2) * BLOCK] = pair[:, HEAD_SIZE:]
    h1_ex[0]()
    hid_p[z] = xfull[z, my_rows]

    doc_start = jnp.int32(0)
    doc_end = jnp.int32(0)
    for i in range(docs_ref.shape[1]):
        doc_end = doc_end + docs_ref[0, i]
        doc_start = jnp.where(doc_end <= c, doc_end, doc_start)
    pairs = window // 2
    wide = (GROUP_HEADS * BLOCK, 2 * BLOCK)
    query_pos = c * BLOCK + lax.broadcasted_iota(jnp.int32, wide, 0) % BLOCK
    first_key = (c - last) * BLOCK + lax.broadcasted_iota(jnp.int32, wide, 1)

    def keys(g):
        return kv[g * 2 * BLOCK : (g + 1) * 2 * BLOCK, :HEAD_SIZE]

    def values(g):
        return kv[g * 2 * BLOCK : (g + 1) * 2 * BLOCK, HEAD_SIZE:]

    for g in range(pairs - 1, -1, -1):
        for j in (2 * g + 1, 2 * g):
            if j < last:

                @pl.when(c - last + j >= 0)
                def _():
                    kv_copy(last - j).wait_recv()

        block = mm(q_s[...], keys(g), NT) * scale
        key_pos = first_key + g * 2 * BLOCK
        block = jnp.where((key_pos <= query_pos) & (key_pos >= doc_start * BLOCK), block, NEG_FILL)
        scores[g] = block
        both = jnp.maximum(block[:, :BLOCK], block[:, BLOCK:])
        peak[...] = both if g == pairs - 1 else jnp.maximum(peak[...], both)

    top = jnp.max(peak[...], axis=1, keepdims=True)
    for g in range(pairs):
        e = jnp.exp(scores[g] - top)
        scores[g] = e
        both = e[:, :BLOCK] + e[:, BLOCK:]
        denom[...] = both if g == 0 else denom[...] + both

    inverse = 1.0 / jnp.sum(denom[...], axis=1, keepdims=True)
    for g in range(pairs):
        soft = scores[g] * inverse
        low = soft.astype(BF16)
        scores[g] = soft
        probs[g] = low
        term = mm(low, values(g))
        acc[...] = term if g == 0 else acc[...] + term

    att_s[...] = acc[...].astype(BF16)
    for j in range(GROUP_HEADS):
        att_z[own_z, j * HEAD_SIZE : (j + 1) * HEAD_SIZE] = att_s[j * BLOCK : (j + 1) * BLOCK]
    att_ring[0](1)
    h1_ex[1]()
    h2_ex[0]()
    hid_z[:, t] = hid_p[...]

    sec_copy = remote(gin_ref, cot_loc, sec_s, sec_r, {"section": 1 - s})

    @pl.when(s == 0)
    def _():
        for k in range(2, n_z // 2 + 1):
            att_ring[0](k)
        sec_copy.wait_recv()
        c_ex[0]()

    cotfull[t] = cot_loc[...]
    wo_copy.wait()
    c_ex[1]()
    for j in range(0, GROUP_HEADS, 2):
        pair = project(cotfull, wo, j * HEAD_SIZE, 2 * HEAD_SIZE)
        hc_s[j * BLOCK : (j + 1) * BLOCK] = pair[:, :HEAD_SIZE]
        hc_s[(j + 1) * BLOCK : (j + 2) * BLOCK] = pair[:, HEAD_SIZE:]

    delta = jnp.sum(hc_s[...].astype(F32) * att_s[...].astype(F32), axis=1, keepdims=True)

    def dkv_copy(d):
        return remote(
            dkv_part.at[slot(last - d)], dkv_in.at[d], d_s.at[d], d_r.at[d],
            {"ctx": lax.rem(c - d + n_ctx, n_ctx)},
        )

    for g in range(pairs):
        block = slice(g * 2 * BLOCK, (g + 1) * 2 * BLOCK)
        dprobs = mm(hc_s[...], values(g), NT)
        ds = (scores[g] * (dprobs - delta)).astype(BF16)
        dkv_part[block, :HEAD_SIZE] = (mm(ds, q_s[...], TN) * scale).astype(BF16)
        dkv_part[block, HEAD_SIZE:] = mm(probs[g], hc_s[...], TN).astype(BF16)
        term = mm(ds, keys(g))
        acc[...] = term if g == 0 else acc[...] + term
        for j in (2 * g, 2 * g + 1):
            if j < last:

                @pl.when(c - last + j >= 0)
                def _():
                    dkv_copy(last - j).start()

    for j in range(GROUP_HEADS):
        gq_n[:, j * HEAD_SIZE : (j + 1) * HEAD_SIZE] = (
            acc[j * BLOCK : (j + 1) * BLOCK] * scale
        ).astype(BF16)
    c1_ex[0]()
    gq_z[own_z] = gq_n[...]
    gq_ring[0](1)
    cot_p[z] = cotfull[z, my_rows]

    @pl.loop(0, n_tp)
    def _(p):
        feat_f[p] = mm(gq_n[...], wq[pl.ds(p * part, part), :heads], NT)

    c1_ex[1]()
    c2_ex[0]()
    cot_z[:, t] = cot_p[...]

    @pl.when(s == 0)
    def _():
        gq_ring[0](2)

    acc[:BLOCK] = dkv_part[slot(last), :HEAD_SIZE].astype(F32)
    acc[BLOCK : 2 * BLOCK] = dkv_part[slot(last), HEAD_SIZE:].astype(F32)

    @pl.loop(1, window)
    def _(d):
        @pl.when(c + d < n_ctx)
        def _():
            dkv_copy(d).wait_recv()
            acc[:BLOCK] += dkv_in[d, :, :HEAD_SIZE].astype(F32)
            acc[BLOCK : 2 * BLOCK] += dkv_in[d, :, HEAD_SIZE:].astype(F32)

    gkv_n[:, :HEAD_SIZE] = acc[:BLOCK].astype(BF16)
    gkv_n[:, HEAD_SIZE:] = acc[BLOCK : 2 * BLOCK].astype(BF16)
    gkv_z[own_z] = gkv_n[...]
    gkv_ring[0](1)

    @pl.loop(1, n_tp + 1)
    def _(i):
        p = lax.rem(t + i, n_tp)
        total = feat_f[p] + mm(gkv_n[...], wq[pl.ds(p * part, part), heads:], NT)
        feat_out[p] = total.astype(BF16)

        @pl.when(i < n_tp)
        def _():
            f_ex[3](p).start()

    feat_in[t] = feat_out[t]

    mate = {"ctx": z * 2 + 1 - lo}
    y_copies = [
        remote(y_out_o, y_in_o, y_s.at[0], y_r.at[0], mate),
        remote(y_out_q, y_in_q, y_s.at[1], y_r.at[1], mate),
        remote(y_out_k, y_in_k, y_s.at[2], y_r.at[2], mate),
    ]
    positions = n_z * BLOCK
    theirs = pl.ds(pl.multiple_of((1 - lo) * half, half), half)
    mine = pl.ds(pl.multiple_of(lo * half, half), half)

    def turn(ref):
        turned[...] = ref[...].reshape(positions, part).T

    def weight_part(right, y_out, out, base, copy):
        step = min(256, heads)
        for k in range(0, right.shape[1], step):
            y_out[:, k : k + step] = mm(turned[theirs], right[:, k : k + step]).astype(BF16)
        copy.start()
        for k in range(0, right.shape[1], step):
            out[:, base + k : base + k + step] = mm(turned[mine], right[:, k : k + step])

    def grad_of_out():
        c2_ex[1]()
        att_ring[1]()
        turn(cot_z)
        weight_part(att_z, y_out_o, gout_ref, 0, y_copies[0])
        h2_ex[1]()
        turn(hid_z)

    @pl.when(s == 0)
    def _():
        gq_ring[0](3)
        gkv_ring[0](2)
        grad_of_out()
        gq_ring[0](4)
        gkv_ring[0](3)

    f_ex[1]()
    feature = jnp.zeros((BLOCK, part), F32)
    for p in range(n_tp):
        feature = feature + feat_in[p].astype(F32)
    inv = inv_b[:, :1]
    gain = gain_ref[:, pl.ds(pl.multiple_of(t * part, part), part)]
    scaled = feature * gain
    normed = x_ref[...].astype(F32) * inv
    row_sum = jnp.sum(scaled * normed, axis=1, keepdims=True)
    rs_out[...] = jnp.broadcast_to(row_sum, (BLOCK, BLOCK)).T[:8]
    r_ex[0]()
    rs_in[t] = rs_out[...]
    r_ex[1]()
    total = rs_in[0]
    for p in range(1, n_tp):
        total = total + rs_in[p]
    mean = jnp.broadcast_to(total[:1] / width, (BLOCK, BLOCK)).T[:, :1]
    gin_ref[...] = (cot_loc[...].astype(F32) + inv * (scaled - normed * mean)).astype(BF16)

    @pl.when(s == 1)
    def _():
        sec_copy.start()

    @pl.when(s == 0)
    def _():
        gkv_ring[0](4)

    @pl.when(s == 1)
    def _():
        for k in range(2, n_z // 2 + 1):
            att_ring[0](k)
            gq_ring[0](k)
            gkv_ring[0](k)
        grad_of_out()

    gq_ring[1]()
    weight_part(gq_z, y_out_q, gqkv_ref, 0, y_copies[1])
    gkv_ring[1]()
    weight_part(gkv_z, y_out_k, gqkv_ref, heads, y_copies[2])
    for y_in, out, base, copy in (
        (y_in_o, gout_ref, 0, y_copies[0]),
        (y_in_q, gqkv_ref, 0, y_copies[1]),
        (y_in_k, gqkv_ref, heads, y_copies[2]),
    ):
        copy.wait_recv()
        out[:, base : base + y_in.shape[1]] += y_in[...].astype(F32)

    for ex in (x_ex, c_ex, f_ex, r_ex, h1_ex, h2_ex, c1_ex, c2_ex, att_ring, gq_ring, gkv_ring):
        ex[2]()
    for copy in y_copies:
        copy.wait_send()

    @pl.loop(1, window)
    def _(d):
        @pl.when(c + d < n_ctx)
        def _():
            kv_copy(d).wait_send()

        @pl.when(c - d >= 0)
        def _():
            dkv_copy(d).wait_send()

    @pl.when(s == 1)
    def _():
        sec_copy.wait_send()


def settle(a_in, b_in, c_in, a_out, b_out, c_out, sem):
    copies = [
        pltpu.make_async_copy(source, target, sem.at[i])
        for i, (source, target) in enumerate(((a_in, a_out), (b_in, b_out), (c_in, c_out)))
    ]
    for copy in copies:
        copy.start()
    for copy in copies:
        copy.wait()


def body(layer_input, loss_cot, token_weights, doc_blocks, norm_gain, qkv_weight, out_weight):
    n_ctx, n_tp = lax.axis_size("ctx"), lax.axis_size("tp")
    n_z = n_ctx // 2
    part = layer_input.shape[3]
    width = part * n_tp
    cols, heads = qkv_weight.shape[2], out_weight.shape[2]
    window = min(MAX_DOC, n_ctx)
    q_rows = GROUP_HEADS * BLOCK
    kv_cols = 2 * HEAD_SIZE
    half = part // 2
    share = BLOCK // n_tp
    vmem = lambda shape, dtype=BF16: pltpu.VMEM(shape, dtype)
    dma = lambda *n: pltpu.SemaphoreType.DMA(n)
    scratch = [
        vmem((width, cols)), vmem((width, heads)),
        vmem((n_tp, BLOCK, part)), vmem((n_tp, BLOCK, part)), vmem((BLOCK, part)), vmem((BLOCK, BLOCK), F32),
        vmem((window * BLOCK, kv_cols)),
        vmem((q_rows, HEAD_SIZE)), vmem((q_rows, HEAD_SIZE)), vmem((q_rows, HEAD_SIZE)),
        vmem((BLOCK, heads)), vmem((BLOCK, kv_cols)),
        vmem((window // 2, q_rows, 2 * BLOCK), F32), vmem((window // 2, q_rows, 2 * BLOCK)),
        vmem((q_rows, BLOCK), F32), vmem((q_rows, BLOCK), F32), vmem((q_rows, HEAD_SIZE), F32),
        vmem((window * BLOCK, kv_cols)), vmem((window, BLOCK, kv_cols)),
        vmem((n_tp, BLOCK, part), F32), vmem((n_tp, BLOCK, part)), vmem((n_tp, BLOCK, part)),
        vmem((8, BLOCK), F32), vmem((n_tp, 8, BLOCK), F32),
        vmem((n_z, share, part)), vmem((n_z, share, part)),
        vmem((n_z, n_tp, share, part)), vmem((n_z, n_tp, share, part)), vmem((n_z * BLOCK, heads)),
        vmem((n_z * BLOCK, heads)), vmem((n_z * BLOCK, kv_cols)), vmem((part, n_z * BLOCK)),
        vmem((half, heads)), vmem((half, heads)), vmem((half, kv_cols)),
        vmem((half, heads)), vmem((half, heads)), vmem((half, kv_cols)),
        dma(2), dma(n_tp), dma(n_tp), dma(n_tp), dma(n_tp), dma(window), dma(window), dma(window), dma(window),
        dma(n_tp), dma(n_tp), dma(n_tp), dma(n_tp),
        dma(n_z), dma(n_z), dma(n_tp), dma(n_tp), dma(n_z), dma(n_z), dma(n_tp), dma(n_tp),
        dma(n_z), dma(n_z), dma(n_z), dma(n_z), dma(n_z), dma(n_z),
        dma(3), dma(3), pltpu.SemaphoreType.DMA, pltpu.SemaphoreType.DMA, pltpu.SemaphoreType.REGULAR,
    ]
    in_vmem = pl.BlockSpec(memory_space=pltpu.VMEM)
    anywhere = pl.BlockSpec(memory_space=pl.ANY)
    grad_in, grad_qkv, grad_out = pl.pallas_call(
        functools.partial(kernel, n_ctx, n_tp, window),
        out_shape=(
            jax.ShapeDtypeStruct((BLOCK, part), BF16),
            jax.ShapeDtypeStruct((half, cols), F32),
            jax.ShapeDtypeStruct((half, heads), F32),
        ),
        in_specs=[
            in_vmem, in_vmem, in_vmem, pl.BlockSpec(memory_space=pltpu.SMEM), in_vmem, anywhere, anywhere,
        ],
        out_specs=(in_vmem, in_vmem, in_vmem),
        scratch_shapes=scratch,
        compiler_params=pltpu.CompilerParams(
            collective_id=0, has_side_effects=True, vmem_limit_bytes=56 * 1024 * 1024
        ),
    )(
        layer_input[0, 0], loss_cot[0], token_weights, doc_blocks, norm_gain, qkv_weight[0], out_weight[0]
    )
    results = (grad_in, grad_qkv, grad_out)
    grad_in, grad_qkv, grad_out = pl.pallas_call(
        settle,
        out_shape=tuple(jax.ShapeDtypeStruct(r.shape, r.dtype) for r in results),
        in_specs=[anywhere] * 3,
        out_specs=(anywhere,) * 3,
        scratch_shapes=[dma(3)],
    )(*results)
    return grad_in[None, None], grad_qkv[None], grad_out[None]


def solution(mesh):
    placed = (
        P("section", None, "ctx", "tp"),
        P(None, "ctx", "tp"),
        P(None, "ctx"),
        P(),
        P("section", None),
        P("section", None, "tp"),
        P("section", None, "tp"),
    )
    return jax.shard_map(
        body,
        mesh=mesh,
        in_specs=placed,
        out_specs=(
            P("section", None, "ctx", "tp"),
            P("section", "ctx", "tp"),
            P("section", "ctx", "tp"),
        ),
        check_vma=False,
    )
```

time: 176 us -> 185 us (1.051)
  Pallas kernels: 167 us -> 183 us
  local copies, waits for them, and re-layouts: 5.5 us -> 0 us
    pallas_call x0 -> x1, Pallas kernels: none -> 44.8 us  [body(): pl.pallas_call(settle, out_shape=tuple((jax.ShapeDtypeStruct(r.shape, r.d...]
    pallas_call x1, Pallas kernels: 167 us -> 138 us  [body(): pl.pallas_call(functools.partial(kernel, n_ctx, n_tp, window), out_shape=...]
    unnamed x3 -> x0, local copies, waits for them, and re-layouts: 5.5 us -> none
where the time goes in v2:
time: 185 us; the launch traced here: 183 us
  Pallas kernels  183 us (99%)
    pallas_call x1, Pallas kernels, body(): pl.pallas_call(functools.partial(kernel, n_ctx, n_tp, window), out_shape=...  138 us
    pallas_call x1, Pallas kernels, body(): pl.pallas_call(settle, out_shape=tuple((jax.ShapeDtypeStruct(r.shape, r.d...  44.8 us

profile of v2, /device:TPU:2, one launch (start us, length us, event | category | flops | bytes accessed | tf_op | source)
XLA Modules:
  0.0 183.3 jit_solution(11301417876448106774)
XLA Ops:
  0.6 137.9 %shard_map.94 = (bf16[128,512]{1,0:T(8,128)(2,1)}, f32[256,768]{1,0:T(8,128)}, f32[256,512]{1,0:T(8,128)}) custom-call(bf16[128,512]{1,0:T(8,128)(2,1)} %bitcast.9, bf16[128,512]{1,0:T(8,128)(2,1)} %bitcast.10, s32[1,128]{1,0:T(1,128)} %tw_ref.1, s32[1,3]{1,0:T(1,128)} %docs_ref.1, f32[1,4096]{1,0:T(1,128)} %gain_ref.1, bf16[4096,768]{1,0:T(8,128)(2,1)} %bitcast.7, ...), custom_call_target="tpu_custom_call" | custom-call | tf_op jit(solution)/shard_map/pallas_call | solution.py:518
  138.5 44.8 %shard_map.95 = (bf16[128,512]{1,0:T(8,128)(2,1)}, f32[256,768]{1,0:T(8,128)}, f32[256,512]{1,0:T(8,128)}) custom-call(bf16[128,512]{1,0:T(8,128)(2,1)} %get-tuple-element.9.a_in, f32[256,768]{1,0:T(8,128)} %get-tuple-element.10.b_in, f32[256,512]{1,0:T(8,128)} %get-tuple-element.11.c_in), custom_call_target="tpu_custom_call" | custom-call | tf_op jit(solution)/shard_map/pallas_call | solution.py:537

commit v3 on v2

--- a/solution.py
+++ b/solution.py
@@ -31,12 +31,12 @@
     x_ref, loss_ref, tw_ref, docs_ref, gain_ref, wq_hbm, wo_hbm,
     gin_ref, gqkv_ref, gout_ref,
     wq, wo, xfull, cotfull, cot_loc, inv_b,
-    kv, q_s, hc_s, att_s, gq_n, gkv_n, scores, probs, peak, denom, acc,
+    kv, q_s, hc_s, att_s, gq_n, gkv_n, scores, probs, dscores, peak, denom, acc, row_acc,
     dkv_part, dkv_in, feat_f, feat_out, feat_in, rs_out, rs_in,
     hid_p, cot_p, hid_z, cot_z, att_z, gq_z, gkv_z, turned,
     y_out_o, y_out_q, y_out_k, y_in_o, y_in_q, y_in_k,
-    w_sem, x_s, x_r, c_s, c_r, kv_s, kv_r, d_s, d_r, f_s, f_r, r_s, r_r,
-    h1_s, h1_r, h2_s, h2_r, c1_s, c1_r, c2_s, c2_r, az_s, az_r, qz_s, qz_r, kz_s, kz_r, y_s, y_r, sec_s, sec_r, gate,
+    w_sem, x_s, x_r, c_s, c_r, kv_s, kv_r, kv_f, d_s, d_r, f_s, f_r, r_s, r_r,
+    h1_s, h1_r, h2_s, h2_r, c1_s, c1_r, c2_s, c2_r, az_s, az_r, qz_s, qz_r, kz_s, kz_r, y_s, y_r, sec_s, gate,
 ):
     s = lax.axis_index("section")
     c = lax.axis_index("ctx")
@@ -136,7 +136,7 @@
     c2_ex = exchange(n_tp, t, tp_dev, whole(cot_p), lambda p: cot_z.at[:, p], c2_s, c2_r)
     att_ring = ring(att_z, az_s, az_r)
     gq_ring = ring(gq_z, qz_s, qz_r)
-    gkv_ring = ring(gkv_z, kz_s, kz_r)
+    kz_ex = exchange(n_z, z, z_dev, whole(gkv_n), lambda p: gkv_z.at[pl.ds(p * BLOCK, BLOCK)], kz_s, kz_r)
     own_z = pl.ds(pl.multiple_of(z * BLOCK, BLOCK), BLOCK)
     wq_copy = pltpu.make_async_copy(wq_hbm, wq, w_sem.at[0])
     wo_copy = pltpu.make_async_copy(wo_hbm, wo, w_sem.at[1])
@@ -155,8 +155,11 @@
     def _(i):
         pl.semaphore_signal(barrier, inc=1, device_id={"ctx": lax.rem(c + i, n_ctx)}, device_id_type=MESH)
 
-    pl.semaphore_signal(barrier, inc=1, device_id={"section": 1 - s}, device_id_type=MESH)
-    pl.semaphore_wait(barrier, n_tp + n_ctx - 1)
+    @pl.loop(0, n_tp)
+    def _(p):
+        pl.semaphore_signal(barrier, inc=1, device_id={"section": 1 - s, "tp": p}, device_id_type=MESH)
+
+    pl.semaphore_wait(barrier, 2 * n_tp + n_ctx - 2)
 
     @pl.when(s == 0)
     def _():
@@ -169,6 +172,7 @@
     def _():
         weights = jnp.broadcast_to(tw_ref[...].astype(F32), (BLOCK, BLOCK)).T[:, :1]
         cot_loc[...] = (loss_ref[...].astype(F32) * weights).astype(BF16)
+        cotfull[t] = cot_loc[...]
         c_ex[0]()
 
     x_ex[1]()
@@ -201,16 +205,48 @@
     wq_copy.wait()
     kv[slot(last)] = project(xfull, wq, heads, 2 * HEAD_SIZE)
 
-    def kv_copy(d):
+    steps_z = (window - 1) // 2 + 1
+    mate = {"ctx": z * 2 + 1 - lo}
+    far = window - 1
+
+    def kv_up(k):
         return remote(
-            kv.at[slot(last)], kv.at[slot(last - d)], kv_s.at[d], kv_r.at[d], {"ctx": lax.rem(c + d, n_ctx)}
+            kv.at[slot(last)], kv.at[slot(last - 2 * k)], kv_s.at[2 * k], kv_r.at[2 * k],
+            {"ctx": lax.rem(c + 2 * k, n_ctx)},
         )
 
-    @pl.loop(1, window)
-    def _(d):
-        @pl.when(c + d < n_ctx)
+    def kv_on(k):
+        away = 2 * k + 1 - 2 * lo
+        return remote(
+            kv.at[slot(last - 2 * k)], kv.at[slot(last - away)], kv_s.at[2 * k + 1], kv_r.at[away], mate
+        )
+
+    def kv_far():
+        return remote(
+            kv.at[slot(last)], kv.at[slot(last - far)], kv_f.at[0], kv_r.at[far],
+            {"ctx": lax.rem(c + far, n_ctx)},
+        )
+
+    def kv_arrival(d):
+        return remote(
+            kv.at[slot(last - d)], kv.at[slot(last - d)], kv_s.at[0], kv_r.at[d], mate
+        )
+
+    @pl.loop(1, steps_z)
+    def _(i):
+        k = steps_z - i
+
+        @pl.when(z + k < n_z)
         def _():
-            kv_copy(d).start()
+            kv_up(k).start()
+
+    @pl.when((lo == 1) & (c + far < n_ctx))
+    def _():
+        kv_far().start()
+
+    @pl.when(lo == 0)
+    def _():
+        kv_on(0).start()
 
     for j in range(0, GROUP_HEADS, 2):
         pair = project(xfull, wq, j * HEAD_SIZE, 2 * HEAD_SIZE)
@@ -218,6 +254,34 @@
         q_s[(j + 1) * BLOCK : (j + 2) * BLOCK] = pair[:, HEAD_SIZE:]
     h1_ex[0]()
     hid_p[z] = xfull[z, my_rows]
+
+    def pass_hidden():
+        h1_ex[1]()
+        h2_ex[0]()
+        hid_z[:, t] = hid_p[...]
+
+    def head_cotangent():
+        wo_copy.wait()
+        for j in range(0, GROUP_HEADS, 2):
+            pair = project(cotfull, wo, j * HEAD_SIZE, 2 * HEAD_SIZE)
+            hc_s[j * BLOCK : (j + 1) * BLOCK] = pair[:, :HEAD_SIZE]
+            hc_s[(j + 1) * BLOCK : (j + 2) * BLOCK] = pair[:, HEAD_SIZE:]
+
+    @pl.loop(1, steps_z)
+    def _(k):
+        @pl.when(z - k >= 0)
+        def _():
+            kv_up(k).wait_recv()
+            kv_on(k).start()
+
+    @pl.when(s == 0)
+    def _():
+        pass_hidden()
+
+    @pl.when(s == 1)
+    def _():
+        c_ex[1]()
+        head_cotangent()
 
     doc_start = jnp.int32(0)
     doc_end = jnp.int32(0)
@@ -239,9 +303,11 @@
         for j in (2 * g + 1, 2 * g):
             if j < last:
 
-                @pl.when(c - last + j >= 0)
-                def _():
-                    kv_copy(last - j).wait_recv()
+                if (last - j) % 2 == 1:
+
+                    @pl.when(c - last + j >= 0)
+                    def _():
+                        kv_arrival(last - j).wait_recv()
 
         block = mm(q_s[...], keys(g), NT) * scale
         key_pos = first_key + g * 2 * BLOCK
@@ -269,27 +335,24 @@
     att_s[...] = acc[...].astype(BF16)
     for j in range(GROUP_HEADS):
         att_z[own_z, j * HEAD_SIZE : (j + 1) * HEAD_SIZE] = att_s[j * BLOCK : (j + 1) * BLOCK]
-    att_ring[0](1)
-    h1_ex[1]()
-    h2_ex[0]()
-    hid_z[:, t] = hid_p[...]
-
-    sec_copy = remote(gin_ref, cot_loc, sec_s, sec_r, {"section": 1 - s})
+
+    def sec_copy(p):
+        return remote(gin_ref, cotfull.at[t], sec_s.at[p], c_r.at[t], {"section": 1 - s, "tp": p})
+
+    @pl.when(s == 1)
+    def _():
+        pass_hidden()
 
     @pl.when(s == 0)
     def _():
-        for k in range(2, n_z // 2 + 1):
+        for k in range(1, n_z // 2 + 1):
             att_ring[0](k)
-        sec_copy.wait_recv()
-        c_ex[0]()
-
-    cotfull[t] = cot_loc[...]
-    wo_copy.wait()
-    c_ex[1]()
-    for j in range(0, GROUP_HEADS, 2):
-        pair = project(cotfull, wo, j * HEAD_SIZE, 2 * HEAD_SIZE)
-        hc_s[j * BLOCK : (j + 1) * BLOCK] = pair[:, :HEAD_SIZE]
-        hc_s[(j + 1) * BLOCK : (j + 2) * BLOCK] = pair[:, HEAD_SIZE:]
+
+        @pl.loop(0, n_tp)
+        def _(p):
+            remote(cotfull.at[p], cotfull.at[p], sec_s.at[p], c_r.at[p], {"section": 1 - s}).wait_recv()
+
+        head_cotangent()
 
     delta = jnp.sum(hc_s[...].astype(F32) * att_s[...].astype(F32), axis=1, keepdims=True)
 
@@ -305,8 +368,7 @@
         ds = (scores[g] * (dprobs - delta)).astype(BF16)
         dkv_part[block, :HEAD_SIZE] = (mm(ds, q_s[...], TN) * scale).astype(BF16)
         dkv_part[block, HEAD_SIZE:] = mm(probs[g], hc_s[...], TN).astype(BF16)
-        term = mm(ds, keys(g))
-        acc[...] = term if g == 0 else acc[...] + term
+        dscores[g] = ds
         for j in (2 * g, 2 * g + 1):
             if j < last:
 
@@ -314,25 +376,37 @@
                 def _():
                     dkv_copy(last - j).start()
 
+    total = mm(dscores[0], keys(0))
+    for g in range(1, pairs):
+        total = total + mm(dscores[g], keys(g))
+    acc[...] = total
     for j in range(GROUP_HEADS):
         gq_n[:, j * HEAD_SIZE : (j + 1) * HEAD_SIZE] = (
             acc[j * BLOCK : (j + 1) * BLOCK] * scale
         ).astype(BF16)
-    c1_ex[0]()
     gq_z[own_z] = gq_n[...]
-    gq_ring[0](1)
-    cot_p[z] = cotfull[z, my_rows]
+
+    def send_cot():
+        c1_ex[0]()
+        cot_p[z] = cotfull[z, my_rows]
+
+    def pass_cot():
+        c1_ex[1]()
+        c2_ex[0]()
+        cot_z[:, t] = cot_p[...]
+
+    @pl.when(s == 0)
+    def _():
+        send_cot()
+        gq_ring[0](1)
 
     @pl.loop(0, n_tp)
     def _(p):
         feat_f[p] = mm(gq_n[...], wq[pl.ds(p * part, part), :heads], NT)
 
-    c1_ex[1]()
-    c2_ex[0]()
-    cot_z[:, t] = cot_p[...]
-
     @pl.when(s == 0)
     def _():
+        pass_cot()
         gq_ring[0](2)
 
     acc[:BLOCK] = dkv_part[slot(last), :HEAD_SIZE].astype(F32)
@@ -349,21 +423,27 @@
     gkv_n[:, :HEAD_SIZE] = acc[:BLOCK].astype(BF16)
     gkv_n[:, HEAD_SIZE:] = acc[BLOCK : 2 * BLOCK].astype(BF16)
     gkv_z[own_z] = gkv_n[...]
-    gkv_ring[0](1)
+    kz_ex[0]()
+    row_acc[...] = jnp.zeros_like(row_acc)
 
     @pl.loop(1, n_tp + 1)
     def _(i):
         p = lax.rem(t + i, n_tp)
         total = feat_f[p] + mm(gkv_n[...], wq[pl.ds(p * part, part), heads:], NT)
-        feat_out[p] = total.astype(BF16)
+        total = total.astype(BF16)
+        feat_out[p] = total
+        row_acc[...] += total.astype(F32) * xfull[p].astype(F32)
 
         @pl.when(i < n_tp)
         def _():
             f_ex[3](p).start()
 
+    row_sum = jnp.sum(row_acc[...], axis=1, keepdims=True)
+    rs_out[...] = jnp.broadcast_to(row_sum, (BLOCK, BLOCK)).T[:8]
+    r_ex[0]()
+    rs_in[t] = rs_out[...]
     feat_in[t] = feat_out[t]
 
-    mate = {"ctx": z * 2 + 1 - lo}
     y_copies = [
         remote(y_out_o, y_in_o, y_s.at[0], y_r.at[0], mate),
         remote(y_out_q, y_in_q, y_s.at[1], y_r.at[1], mate),
@@ -389,18 +469,22 @@
         att_ring[1]()
         turn(cot_z)
         weight_part(att_z, y_out_o, gout_ref, 0, y_copies[0])
+
+    def grad_of_query():
         h2_ex[1]()
         turn(hid_z)
+        gq_ring[1]()
+        weight_part(gq_z, y_out_q, gqkv_ref, 0, y_copies[1])
 
     @pl.when(s == 0)
     def _():
         gq_ring[0](3)
-        gkv_ring[0](2)
         grad_of_out()
         gq_ring[0](4)
-        gkv_ring[0](3)
+        grad_of_query()
 
     f_ex[1]()
+    r_ex[1]()
     feature = jnp.zeros((BLOCK, part), F32)
     for p in range(n_tp):
         feature = feature + feat_in[p].astype(F32)
@@ -408,36 +492,28 @@
     gain = gain_ref[:, pl.ds(pl.multiple_of(t * part, part), part)]
     scaled = feature * gain
     normed = x_ref[...].astype(F32) * inv
-    row_sum = jnp.sum(scaled * normed, axis=1, keepdims=True)
-    rs_out[...] = jnp.broadcast_to(row_sum, (BLOCK, BLOCK)).T[:8]
-    r_ex[0]()
-    rs_in[t] = rs_out[...]
-    r_ex[1]()
     total = rs_in[0]
     for p in range(1, n_tp):
         total = total + rs_in[p]
     mean = jnp.broadcast_to(total[:1] / width, (BLOCK, BLOCK)).T[:, :1]
-    gin_ref[...] = (cot_loc[...].astype(F32) + inv * (scaled - normed * mean)).astype(BF16)
+    gin_ref[...] = (cotfull[t].astype(F32) + inv * (scaled - normed * mean)).astype(BF16)
 
     @pl.when(s == 1)
     def _():
-        sec_copy.start()
-
-    @pl.when(s == 0)
-    def _():
-        gkv_ring[0](4)
-
-    @pl.when(s == 1)
-    def _():
-        for k in range(2, n_z // 2 + 1):
+        @pl.loop(0, n_tp)
+        def _(i):
+            sec_copy(lax.rem(t + 1 + i, n_tp)).start()
+
+        send_cot()
+        for k in range(1, n_z // 2 + 1):
             att_ring[0](k)
             gq_ring[0](k)
-            gkv_ring[0](k)
+            if k == 2 or n_z == 2:
+                pass_cot()
         grad_of_out()
-
-    gq_ring[1]()
-    weight_part(gq_z, y_out_q, gqkv_ref, 0, y_copies[1])
-    gkv_ring[1]()
+        grad_of_query()
+
+    kz_ex[1]()
     weight_part(gkv_z, y_out_k, gqkv_ref, heads, y_copies[2])
     for y_in, out, base, copy in (
         (y_in_o, gout_ref, 0, y_copies[0]),
@@ -447,24 +523,42 @@
         copy.wait_recv()
         out[:, base : base + y_in.shape[1]] += y_in[...].astype(F32)
 
-    for ex in (x_ex, c_ex, f_ex, r_ex, h1_ex, h2_ex, c1_ex, c2_ex, att_ring, gq_ring, gkv_ring):
+    for ex in (x_ex, f_ex, r_ex, h1_ex, h2_ex, c1_ex, c2_ex, kz_ex, att_ring, gq_ring):
         ex[2]()
     for copy in y_copies:
         copy.wait_send()
 
+    @pl.loop(1, steps_z)
+    def _(k):
+        @pl.when(z + k < n_z)
+        def _():
+            kv_up(k).wait_send()
+
+        @pl.when(z - k >= 0)
+        def _():
+            kv_on(k).wait_send()
+
+    @pl.when((lo == 1) & (c + far < n_ctx))
+    def _():
+        kv_far().wait_send()
+
+    @pl.when(lo == 0)
+    def _():
+        kv_on(0).wait_send()
+
     @pl.loop(1, window)
     def _(d):
-        @pl.when(c + d < n_ctx)
-        def _():
-            kv_copy(d).wait_send()
-
         @pl.when(c - d >= 0)
         def _():
             dkv_copy(d).wait_send()
 
     @pl.when(s == 1)
     def _():
-        sec_copy.wait_send()
+        c_ex[2]()
+
+        @pl.loop(0, n_tp)
+        def _(p):
+            sec_copy(p).wait_send()
 
 
 def settle(a_in, b_in, c_in, a_out, b_out, c_out, sem):
@@ -498,7 +592,8 @@
         vmem((q_rows, HEAD_SIZE)), vmem((q_rows, HEAD_SIZE)), vmem((q_rows, HEAD_SIZE)),
         vmem((BLOCK, heads)), vmem((BLOCK, kv_cols)),
         vmem((window // 2, q_rows, 2 * BLOCK), F32), vmem((window // 2, q_rows, 2 * BLOCK)),
-        vmem((q_rows, BLOCK), F32), vmem((q_rows, BLOCK), F32), vmem((q_rows, HEAD_SIZE), F32),
+        vmem((window // 2, q_rows, 2 * BLOCK)),
+        vmem((q_rows, BLOCK), F32), vmem((q_rows, BLOCK), F32), vmem((q_rows, HEAD_SIZE), F32), vmem((BLOCK, part), F32),
         vmem((window * BLOCK, kv_cols)), vmem((window, BLOCK, kv_cols)),
         vmem((n_tp, BLOCK, part), F32), vmem((n_tp, BLOCK, part)), vmem((n_tp, BLOCK, part)),
         vmem((8, BLOCK), F32), vmem((n_tp, 8, BLOCK), F32),
@@ -507,11 +602,11 @@
         vmem((n_z * BLOCK, heads)), vmem((n_z * BLOCK, kv_cols)), vmem((part, n_z * BLOCK)),
         vmem((half, heads)), vmem((half, heads)), vmem((half, kv_cols)),
         vmem((half, heads)), vmem((half, heads)), vmem((half, kv_cols)),
-        dma(2), dma(n_tp), dma(n_tp), dma(n_tp), dma(n_tp), dma(window), dma(window), dma(window), dma(window),
+        dma(2), dma(n_tp), dma(n_tp), dma(n_tp), dma(n_tp), dma(window), dma(window), dma(1), dma(window), dma(window),
         dma(n_tp), dma(n_tp), dma(n_tp), dma(n_tp),
         dma(n_z), dma(n_z), dma(n_tp), dma(n_tp), dma(n_z), dma(n_z), dma(n_tp), dma(n_tp),
         dma(n_z), dma(n_z), dma(n_z), dma(n_z), dma(n_z), dma(n_z),
-        dma(3), dma(3), pltpu.SemaphoreType.DMA, pltpu.SemaphoreType.DMA, pltpu.SemaphoreType.REGULAR,
+        dma(3), dma(3), dma(n_tp), pltpu.SemaphoreType.REGULAR,
     ]
     in_vmem = pl.BlockSpec(memory_space=pltpu.VMEM)
     anywhere = pl.BlockSpec(memory_space=pl.ANY)
@@ -537,7 +632,7 @@
     grad_in, grad_qkv, grad_out = pl.pallas_call(
         settle,
         out_shape=tuple(jax.ShapeDtypeStruct(r.shape, r.dtype) for r in results),
-        in_specs=[anywhere] * 3,
+        in_specs=[in_vmem] * 3,
         out_specs=(anywhere,) * 3,
         scratch_shapes=[dma(3)],
     )(*results)

time: 185 us -> 126 us (0.68)
  Pallas kernels: 183 us -> 124 us
    pallas_call x1, Pallas kernels: 44.8 us -> 2.44 us  [body(): pl.pallas_call(settle, out_shape=tuple((jax.ShapeDtypeStruct(r.shape, r.d...]
    pallas_call x1, Pallas kernels: 138 us -> 122 us  [body(): pl.pallas_call(functools.partial(kernel, n_ctx, n_tp, window), out_shape=...]
where the time goes in v3:
time: 126 us; the launch traced here: 125 us
  Pallas kernels  124 us (98%)
    pallas_call x1, Pallas kernels, body(): pl.pallas_call(functools.partial(kernel, n_ctx, n_tp, window), out_shape=...  122 us

profile of v3, /device:TPU:2, one launch (start us, length us, event | category | flops | bytes accessed | tf_op | source)
XLA Modules:
  0.0 125.0 jit_solution(11431851474101824718)
XLA Ops:
  0.6 121.9 %shard_map.94 = (bf16[128,512]{1,0:T(8,128)(2,1)}, f32[256,768]{1,0:T(8,128)}, f32[256,512]{1,0:T(8,128)}) custom-call(bf16[128,512]{1,0:T(8,128)(2,1)} %bitcast.9, bf16[128,512]{1,0:T(8,128)(2,1)} %bitcast.10, s32[1,128]{1,0:T(1,128)} %tw_ref.1, s32[1,3]{1,0:T(1,128)} %docs_ref.1, f32[1,4096]{1,0:T(1,128)} %gain_ref.1, bf16[4096,768]{1,0:T(8,128)(2,1)} %bitcast.7, ...), custom_call_target="tpu_custom_call" | custom-call | tf_op jit(solution)/shard_map/pallas_call | solution.py:613
  122.6 2.4 %shard_map.95 = (bf16[128,512]{1,0:T(8,128)(2,1)}, f32[256,768]{1,0:T(8,128)}, f32[256,512]{1,0:T(8,128)}) custom-call(bf16[128,512]{1,0:T(8,128)(2,1)} %get-tuple-element.9.a_in, f32[256,768]{1,0:T(8,128)} %get-tuple-element.10.b_in, f32[256,512]{1,0:T(8,128)} %get-tuple-element.11.c_in), custom_call_target="tpu_custom_call" | custom-call | tf_op jit(solution)/shard_map/pallas_call | solution.py:632

commit v4 on v3

--- a/solution.py
+++ b/solution.py
@@ -31,12 +31,12 @@
     x_ref, loss_ref, tw_ref, docs_ref, gain_ref, wq_hbm, wo_hbm,
     gin_ref, gqkv_ref, gout_ref,
     wq, wo, xfull, cotfull, cot_loc, inv_b,
-    kv, q_s, hc_s, att_s, gq_n, gkv_n, scores, probs, dscores, peak, denom, acc, row_acc,
+    kv, q_s, hc_s, att_s, gq_n, gkv_n, scores, probs, dscores, peak, denom, acc, kv_acc, hc_acc, sq_out, sq_in,
     dkv_part, dkv_in, feat_f, feat_out, feat_in, rs_out, rs_in,
     hid_p, cot_p, hid_z, cot_z, att_z, gq_z, gkv_z, turned,
     y_out_o, y_out_q, y_out_k, y_in_o, y_in_q, y_in_k,
     w_sem, x_s, x_r, c_s, c_r, kv_s, kv_r, kv_f, d_s, d_r, f_s, f_r, r_s, r_r,
-    h1_s, h1_r, h2_s, h2_r, c1_s, c1_r, c2_s, c2_r, az_s, az_r, qz_s, qz_r, kz_s, kz_r, y_s, y_r, sec_s, gate,
+    h1_s, h1_r, h2_s, h2_r, c1_s, c1_r, c2_s, c2_r, az_s, az_r, qz_s, qz_r, kz_s, kz_r, y_s, y_r, sec_s, q_sem, q_rcv, gate,
 ):
     s = lax.axis_index("section")
     c = lax.axis_index("ctx")
@@ -84,7 +84,7 @@
             def _(i):
                 copy_to(lax.rem(me + i, n)).wait_send()
 
-        return start, wait_recv, wait_send, copy_to
+        return start, wait_recv, wait_send, copy_to, copy_from
 
     def ring(ref, ss, rs):
         up, down = z_dev(lax.rem(z + 1, n_z)), z_dev(lax.rem(z + n_z - 1, n_z))
@@ -129,6 +129,7 @@
     x_ex = exchange(n_tp, t, tp_dev, whole(x_ref), lambda p: xfull.at[p], x_s, x_r)
     c_ex = exchange(n_tp, t, tp_dev, whole(cot_loc), lambda p: cotfull.at[p], c_s, c_r)
     f_ex = exchange(n_tp, t, tp_dev, lambda p: feat_out.at[p], lambda p: feat_in.at[p], f_s, f_r)
+    q_ex = exchange(n_tp, t, tp_dev, whole(sq_out), lambda p: sq_in.at[p], q_sem, q_rcv)
     r_ex = exchange(n_tp, t, tp_dev, whole(rs_out), lambda p: rs_in.at[p], r_s, r_r)
     h1_ex = exchange(n_z, z, z_dev, lambda p: xfull.at[p, my_rows], lambda p: hid_p.at[p], h1_s, h1_r)
     h2_ex = exchange(n_tp, t, tp_dev, whole(hid_p), lambda p: hid_z.at[:, p], h2_s, h2_r)
@@ -144,6 +145,9 @@
     wq_copy.start()
     wo_copy.start()
     kv[...] = jnp.zeros_like(kv)
+    own_x = x_ref[...].astype(F32)
+    square_sum = jnp.sum(own_x * own_x, axis=1, keepdims=True)
+    sq_out[...] = jnp.broadcast_to(square_sum, (BLOCK, BLOCK)).T[:8]
 
     barrier = pltpu.get_barrier_semaphore()
 
@@ -165,8 +169,34 @@
     def _():
         pl.semaphore_wait(gate, 1)
 
+    q_ex[0]()
     x_ex[0]()
+    sq_in[t] = sq_out[...]
     xfull[t] = x_ref[...]
+
+    def total_of(ref):
+        total = ref[0]
+        for p in range(1, n_tp):
+            total = total + ref[p]
+        return jnp.broadcast_to(total[:1], (BLOCK, BLOCK)).T
+
+    q_ex[1]()
+    inv_b[...] = lax.rsqrt(total_of(sq_in) / width + EPSILON)
+    kv_acc[...] = jnp.zeros_like(kv_acc)
+    wq_copy.wait()
+
+    @pl.loop(0, n_tp)
+    def _(i):
+        p = lax.rem(t - i + n_tp, n_tp)
+
+        @pl.when(i > 0)
+        def _():
+            x_ex[4](p).wait_recv()
+
+        gain = gain_ref[:, pl.ds(pl.multiple_of(p * part, part), part)]
+        hidden = ((xfull[p].astype(F32) * inv_b[:, :1]) * gain).astype(BF16)
+        xfull[p] = hidden
+        kv_acc[...] += mm(hidden, wq[pl.ds(pl.multiple_of(p * part, part), part), heads:])
 
     @pl.when(s == 1)
     def _():
@@ -174,22 +204,6 @@
         cot_loc[...] = (loss_ref[...].astype(F32) * weights).astype(BF16)
         cotfull[t] = cot_loc[...]
         c_ex[0]()
-
-    x_ex[1]()
-
-    @pl.when(s == 1)
-    def _():
-        pl.semaphore_signal(gate, inc=1, device_id={"section": 1 - s}, device_id_type=MESH)
-
-    square = jnp.zeros((BLOCK, part), F32)
-    for p in range(n_tp):
-        wide = xfull[p].astype(F32)
-        square = square + wide * wide
-    inv = lax.rsqrt(jnp.sum(square, axis=1, keepdims=True) / width + EPSILON)
-    inv_b[...] = jnp.broadcast_to(inv, inv_b.shape)
-    for p in range(n_tp):
-        gain = gain_ref[:, p * part : (p + 1) * part]
-        xfull[p] = ((xfull[p].astype(F32) * inv) * gain).astype(BF16)
 
     def project(full, weight, lo_col, n_col):
         total = jnp.zeros((BLOCK, n_col), F32)
@@ -202,8 +216,7 @@
             return pl.ds(j * BLOCK, BLOCK)
         return pl.ds(pl.multiple_of(j * BLOCK, BLOCK), BLOCK)
 
-    wq_copy.wait()
-    kv[slot(last)] = project(xfull, wq, heads, 2 * HEAD_SIZE)
+    kv[slot(last)] = kv_acc[...].astype(BF16)
 
     steps_z = (window - 1) // 2 + 1
     mate = {"ctx": z * 2 + 1 - lo}
@@ -260,12 +273,18 @@
         h2_ex[0]()
         hid_z[:, t] = hid_p[...]
 
-    def head_cotangent():
+    def head_cotangent(arrival):
         wo_copy.wait()
-        for j in range(0, GROUP_HEADS, 2):
-            pair = project(cotfull, wo, j * HEAD_SIZE, 2 * HEAD_SIZE)
-            hc_s[j * BLOCK : (j + 1) * BLOCK] = pair[:, :HEAD_SIZE]
-            hc_s[(j + 1) * BLOCK : (j + 2) * BLOCK] = pair[:, HEAD_SIZE:]
+        hc_acc[...] = jnp.zeros_like(hc_acc)
+
+        @pl.loop(0, n_tp)
+        def _(i):
+            p = lax.rem(t - i + n_tp, n_tp)
+            arrival(i, p)
+            hc_acc[...] += mm(cotfull[p], wo[pl.ds(pl.multiple_of(p * part, part), part)])
+
+        for j in range(GROUP_HEADS):
+            hc_s[j * BLOCK : (j + 1) * BLOCK] = hc_acc[:, j * HEAD_SIZE : (j + 1) * HEAD_SIZE].astype(BF16)
 
     @pl.loop(1, steps_z)
     def _(k):
@@ -281,7 +300,8 @@
     @pl.when(s == 1)
     def _():
         c_ex[1]()
-        head_cotangent()
+        pl.semaphore_signal(gate, inc=1, device_id={"section": 1 - s}, device_id_type=MESH)
+        head_cotangent(lambda i, p: None)
 
     doc_start = jnp.int32(0)
     doc_end = jnp.int32(0)
@@ -348,11 +368,10 @@
         for k in range(1, n_z // 2 + 1):
             att_ring[0](k)
 
-        @pl.loop(0, n_tp)
-        def _(p):
+        def arrival(i, p):
             remote(cotfull.at[p], cotfull.at[p], sec_s.at[p], c_r.at[p], {"section": 1 - s}).wait_recv()
 
-        head_cotangent()
+        head_cotangent(arrival)
 
     delta = jnp.sum(hc_s[...].astype(F32) * att_s[...].astype(F32), axis=1, keepdims=True)
 
@@ -424,24 +443,28 @@
     gkv_n[:, HEAD_SIZE:] = acc[BLOCK : 2 * BLOCK].astype(BF16)
     gkv_z[own_z] = gkv_n[...]
     kz_ex[0]()
-    row_acc[...] = jnp.zeros_like(row_acc)
+
+    row_sum = gkv_n[:, :HEAD_SIZE].astype(F32) * kv[slot(last), :HEAD_SIZE].astype(F32)
+    row_sum = row_sum + gkv_n[:, HEAD_SIZE:].astype(F32) * kv[slot(last), HEAD_SIZE:].astype(F32)
+    for j in range(GROUP_HEADS):
+        row_sum = row_sum + gq_n[:, j * HEAD_SIZE : (j + 1) * HEAD_SIZE].astype(F32) * q_s[
+            j * BLOCK : (j + 1) * BLOCK
+        ].astype(F32)
+    row_sum = jnp.sum(row_sum, axis=1, keepdims=True)
+    rs_out[...] = jnp.broadcast_to(row_sum, (BLOCK, BLOCK)).T[:8]
+    r_ex[0]()
+    rs_in[t] = rs_out[...]
 
     @pl.loop(1, n_tp + 1)
     def _(i):
         p = lax.rem(t + i, n_tp)
         total = feat_f[p] + mm(gkv_n[...], wq[pl.ds(p * part, part), heads:], NT)
-        total = total.astype(BF16)
-        feat_out[p] = total
-        row_acc[...] += total.astype(F32) * xfull[p].astype(F32)
+        feat_out[p] = total.astype(BF16)
 
         @pl.when(i < n_tp)
         def _():
             f_ex[3](p).start()
 
-    row_sum = jnp.sum(row_acc[...], axis=1, keepdims=True)
-    rs_out[...] = jnp.broadcast_to(row_sum, (BLOCK, BLOCK)).T[:8]
-    r_ex[0]()
-    rs_in[t] = rs_out[...]
     feat_in[t] = feat_out[t]
 
     y_copies = [
@@ -492,17 +515,14 @@
     gain = gain_ref[:, pl.ds(pl.multiple_of(t * part, part), part)]
     scaled = feature * gain
     normed = x_ref[...].astype(F32) * inv
-    total = rs_in[0]
-    for p in range(1, n_tp):
-        total = total + rs_in[p]
-    mean = jnp.broadcast_to(total[:1] / width, (BLOCK, BLOCK)).T[:, :1]
+    mean = total_of(rs_in)[:, :1] / width
     gin_ref[...] = (cotfull[t].astype(F32) + inv * (scaled - normed * mean)).astype(BF16)
 
     @pl.when(s == 1)
     def _():
         @pl.loop(0, n_tp)
         def _(i):
-            sec_copy(lax.rem(t + 1 + i, n_tp)).start()
+            sec_copy(lax.rem(t + i, n_tp)).start()
 
         send_cot()
         for k in range(1, n_z // 2 + 1):
@@ -523,7 +543,7 @@
         copy.wait_recv()
         out[:, base : base + y_in.shape[1]] += y_in[...].astype(F32)
 
-    for ex in (x_ex, f_ex, r_ex, h1_ex, h2_ex, c1_ex, c2_ex, kz_ex, att_ring, gq_ring):
+    for ex in (x_ex, q_ex, f_ex, r_ex, h1_ex, h2_ex, c1_ex, c2_ex, kz_ex, att_ring, gq_ring):
         ex[2]()
     for copy in y_copies:
         copy.wait_send()
@@ -593,7 +613,8 @@
         vmem((BLOCK, heads)), vmem((BLOCK, kv_cols)),
         vmem((window // 2, q_rows, 2 * BLOCK), F32), vmem((window // 2, q_rows, 2 * BLOCK)),
         vmem((window // 2, q_rows, 2 * BLOCK)),
-        vmem((q_rows, BLOCK), F32), vmem((q_rows, BLOCK), F32), vmem((q_rows, HEAD_SIZE), F32), vmem((BLOCK, part), F32),
+        vmem((q_rows, BLOCK), F32), vmem((q_rows, BLOCK), F32), vmem((q_rows, HEAD_SIZE), F32),
+        vmem((BLOCK, kv_cols), F32), vmem((BLOCK, heads), F32), vmem((8, BLOCK), F32), vmem((n_tp, 8, BLOCK), F32),
         vmem((window * BLOCK, kv_cols)), vmem((window, BLOCK, kv_cols)),
         vmem((n_tp, BLOCK, part), F32), vmem((n_tp, BLOCK, part)), vmem((n_tp, BLOCK, part)),
         vmem((8, BLOCK), F32), vmem((n_tp, 8, BLOCK), F32),
@@ -606,7 +627,7 @@
         dma(n_tp), dma(n_tp), dma(n_tp), dma(n_tp),
         dma(n_z), dma(n_z), dma(n_tp), dma(n_tp), dma(n_z), dma(n_z), dma(n_tp), dma(n_tp),
         dma(n_z), dma(n_z), dma(n_z), dma(n_z), dma(n_z), dma(n_z),
-        dma(3), dma(3), dma(n_tp), pltpu.SemaphoreType.REGULAR,
+        dma(3), dma(3), dma(n_tp), dma(n_tp), dma(n_tp), pltpu.SemaphoreType.REGULAR,
     ]
     in_vmem = pl.BlockSpec(memory_space=pltpu.VMEM)
     anywhere = pl.BlockSpec(memory_space=pl.ANY)

time: 126 us -> 133 us (1.056)
  Pallas kernels: 124 us -> 131 us
    pallas_call x1, Pallas kernels: 122 us -> 129 us  [body(): pl.pallas_call(functools.partial(kernel, n_ctx, n_tp, window), out_shape=...]
where the time goes in v4:
time: 133 us; the launch traced here: 132 us
  Pallas kernels  131 us (98%)
    pallas_call x1, Pallas kernels, body(): pl.pallas_call(functools.partial(kernel, n_ctx, n_tp, window), out_shape=...  129 us

profile of v4, /device:TPU:2, one launch (start us, length us, event | category | flops | bytes accessed | tf_op | source)
XLA Modules:
  0.0 131.9 jit_solution(7550377752977095551)
XLA Ops:
  0.6 128.8 %shard_map.94 = (bf16[128,512]{1,0:T(8,128)(2,1)}, f32[256,768]{1,0:T(8,128)}, f32[256,512]{1,0:T(8,128)}) custom-call(bf16[128,512]{1,0:T(8,128)(2,1)} %bitcast.9, bf16[128,512]{1,0:T(8,128)(2,1)} %bitcast.10, s32[1,128]{1,0:T(1,128)} %tw_ref.1, s32[1,3]{1,0:T(1,128)} %docs_ref.1, f32[1,4096]{1,0:T(1,128)} %gain_ref.1, bf16[4096,768]{1,0:T(8,128)(2,1)} %bitcast.7, ...), custom_call_target="tpu_custom_call" | custom-call | tf_op jit(solution)/shard_map/pallas_call | solution.py:634
  129.4 2.4 %shard_map.95 = (bf16[128,512]{1,0:T(8,128)(2,1)}, f32[256,768]{1,0:T(8,128)}, f32[256,512]{1,0:T(8,128)}) custom-call(bf16[128,512]{1,0:T(8,128)(2,1)} %get-tuple-element.9.a_in, f32[256,768]{1,0:T(8,128)} %get-tuple-element.10.b_in, f32[256,512]{1,0:T(8,128)} %get-tuple-element.11.c_in), custom_call_target="tpu_custom_call" | custom-call | tf_op jit(solution)/shard_map/pallas_call | solution.py:653

commit v5 on v4

--- a/solution.py
+++ b/solution.py
@@ -204,6 +204,7 @@
         cot_loc[...] = (loss_ref[...].astype(F32) * weights).astype(BF16)
         cotfull[t] = cot_loc[...]
         c_ex[0]()
+        pl.semaphore_signal(gate, inc=1, device_id={"section": 1 - s}, device_id_type=MESH)
 
     def project(full, weight, lo_col, n_col):
         total = jnp.zeros((BLOCK, n_col), F32)
@@ -300,7 +301,6 @@
     @pl.when(s == 1)
     def _():
         c_ex[1]()
-        pl.semaphore_signal(gate, inc=1, device_id={"section": 1 - s}, device_id_type=MESH)
         head_cotangent(lambda i, p: None)
 
     doc_start = jnp.int32(0)
@@ -365,13 +365,13 @@
 
     @pl.when(s == 0)
     def _():
-        for k in range(1, n_z // 2 + 1):
-            att_ring[0](k)
+        att_ring[0](1)
 
         def arrival(i, p):
             remote(cotfull.at[p], cotfull.at[p], sec_s.at[p], c_r.at[p], {"section": 1 - s}).wait_recv()
 
         head_cotangent(arrival)
+        att_ring[0](2)
 
     delta = jnp.sum(hc_s[...].astype(F32) * att_s[...].astype(F32), axis=1, keepdims=True)
 
@@ -418,6 +418,7 @@
     def _():
         send_cot()
         gq_ring[0](1)
+        att_ring[0](3)
 
     @pl.loop(0, n_tp)
     def _(p):
@@ -427,6 +428,7 @@
     def _():
         pass_cot()
         gq_ring[0](2)
+        att_ring[0](4)
 
     acc[:BLOCK] = dkv_part[slot(last), :HEAD_SIZE].astype(F32)
     acc[BLOCK : 2 * BLOCK] = dkv_part[slot(last), HEAD_SIZE:].astype(F32)

time: 133 us -> 129 us (0.970)
  Pallas kernels: 131 us -> 126 us
    pallas_call x1, Pallas kernels: 129 us -> 124 us  [body(): pl.pallas_call(functools.partial(kernel, n_ctx, n_tp, window), out_shape=...]
where the time goes in v5:
time: 129 us; the launch traced here: 127 us
  Pallas kernels  126 us (98%)
    pallas_call x1, Pallas kernels, body(): pl.pallas_call(functools.partial(kernel, n_ctx, n_tp, window), out_shape=...  124 us

profile of v5, /device:TPU:2, one launch (start us, length us, event | category | flops | bytes accessed | tf_op | source)
XLA Modules:
  0.0 127.0 jit_solution(13860413634290646112)
XLA Ops:
  0.6 123.9 %shard_map.94 = (bf16[128,512]{1,0:T(8,128)(2,1)}, f32[256,768]{1,0:T(8,128)}, f32[256,512]{1,0:T(8,128)}) custom-call(bf16[128,512]{1,0:T(8,128)(2,1)} %bitcast.9, bf16[128,512]{1,0:T(8,128)(2,1)} %bitcast.10, s32[1,128]{1,0:T(1,128)} %tw_ref.1, s32[1,3]{1,0:T(1,128)} %docs_ref.1, f32[1,4096]{1,0:T(1,128)} %gain_ref.1, bf16[4096,768]{1,0:T(8,128)(2,1)} %bitcast.7, ...), custom_call_target="tpu_custom_call" | custom-call | tf_op jit(solution)/shard_map/pallas_call | solution.py:636
  124.5 2.4 %shard_map.95 = (bf16[128,512]{1,0:T(8,128)(2,1)}, f32[256,768]{1,0:T(8,128)}, f32[256,512]{1,0:T(8,128)}) custom-call(bf16[128,512]{1,0:T(8,128)(2,1)} %get-tuple-element.9.a_in, f32[256,768]{1,0:T(8,128)} %get-tuple-element.10.b_in, f32[256,512]{1,0:T(8,128)} %get-tuple-element.11.c_in), custom_call_target="tpu_custom_call" | custom-call | tf_op jit(solution)/shard_map/pallas_call | solution.py:655

commit v6 on v5

--- a/solution.py
+++ b/solution.py
@@ -30,7 +30,7 @@
     n_ctx, n_tp, window,
     x_ref, loss_ref, tw_ref, docs_ref, gain_ref, wq_hbm, wo_hbm,
     gin_ref, gqkv_ref, gout_ref,
-    wq, wo, xfull, cotfull, cot_loc, inv_b,
+    wq, wo, xfull, hfull, cotfull, inv_b,
     kv, q_s, hc_s, att_s, gq_n, gkv_n, scores, probs, dscores, peak, denom, acc, kv_acc, hc_acc, sq_out, sq_in,
     dkv_part, dkv_in, feat_f, feat_out, feat_in, rs_out, rs_in,
     hid_p, cot_p, hid_z, cot_z, att_z, gq_z, gkv_z, turned,
@@ -122,19 +122,98 @@
 
         return stage, lambda: arrive(top), wait_send
 
+    n_x = n_tp // 2
+    ty, tx = t // n_x, lax.rem(t, n_x)
+
+    def at(dy, dx):
+        return (ty if dy == 0 else 1 - ty) * n_x + lax.rem(tx + dx + n_x, n_x)
+
+    near = [at(0, -1), at(0, 1)] if n_x > 1 else []
+    mate_t = at(1, 0)
+    order = [t] + near + [mate_t]
+    if n_x > 1:
+        order = order + [at(1, -1), at(1, 1), at(0, 2), at(1, 2)]
+
+    class Spread:
+        def __init__(self, piece, ss, rs):
+            self.piece, self.ss, self.rs = piece, ss, rs
+            self.sends = [self.move(t, None, 0, t, mate_t)]
+            if n_x > 1:
+                left, right = near
+                self.sends += [
+                    self.move(t, None, 1, t, right),
+                    self.move(t, None, 2, t, left),
+                    self.move(left, 0, 3, left, right),
+                    self.move(right, 1, 4, n_tp, left),
+                    self.move(mate_t, None, 5, mate_t, right),
+                    self.move(mate_t, None, 6, mate_t, left),
+                    self.move(at(1, -1), 0, 7, at(1, -1), right),
+                    self.move(at(1, 1), 1, 8, n_tp + 1, left),
+                ]
+
+        def move(self, p, side, i, r, to):
+            return remote(self.piece(p, side), self.piece(p, side), self.ss.at[i], self.rs.at[r], {"tp": to})
+
+        def arrive(self, p, side=None, r=None):
+            self.move(p, side, 0, p if r is None else r, mate_t).wait_recv()
+
+        def start(self):
+            for copy in self.sends[:3]:
+                copy.start()
+
+        def relay(self):
+            if n_x > 1:
+                for p, copy in zip(near, self.sends[3:5]):
+                    self.arrive(p)
+                    copy.start()
+            self.arrive(mate_t)
+            for copy in self.sends[5:7]:
+                copy.start()
+
+        def relay_far(self):
+            for p, copy in zip((at(1, -1), at(1, 1)), self.sends[7:]):
+                self.arrive(p)
+                copy.start()
+
+        def finish(self):
+            if n_x > 1:
+                for i, p in enumerate((at(0, 2), at(1, 2))):
+                    self.arrive(p, 0)
+                    self.arrive(p, 1, n_tp + i)
+
+        def wait_send(self, first=0):
+            for copy in self.sends[first:]:
+                copy.wait_send()
+
+    def block_of(ref):
+        part_rows = BLOCK // 2
+
+        def piece(p, side):
+            return ref.at[p] if side is None else ref.at[p, pl.ds(side * part_rows, part_rows)]
+
+        return piece
+
+    def slice_of(ref):
+        depth = n_z // 2
+
+        def piece(p, side):
+            return ref.at[:, p] if side is None else ref.at[pl.ds(side * depth, depth), p]
+
+        return piece
+
     whole = lambda ref: lambda p: ref
     share = BLOCK // n_tp
     my_rows = pl.ds(pl.multiple_of(t * share, share), share)
 
-    x_ex = exchange(n_tp, t, tp_dev, whole(x_ref), lambda p: xfull.at[p], x_s, x_r)
-    c_ex = exchange(n_tp, t, tp_dev, whole(cot_loc), lambda p: cotfull.at[p], c_s, c_r)
+    x_ag = Spread(block_of(xfull), x_s, x_r)
+    c_ag = Spread(block_of(cotfull), c_s, c_r)
+    h2_ag = Spread(slice_of(hid_z), h2_s, h2_r)
+    c2_ag = Spread(slice_of(cot_z), c2_s, c2_r)
     f_ex = exchange(n_tp, t, tp_dev, lambda p: feat_out.at[p], lambda p: feat_in.at[p], f_s, f_r)
     q_ex = exchange(n_tp, t, tp_dev, whole(sq_out), lambda p: sq_in.at[p], q_sem, q_rcv)
     r_ex = exchange(n_tp, t, tp_dev, whole(rs_out), lambda p: rs_in.at[p], r_s, r_r)
-    h1_ex = exchange(n_z, z, z_dev, lambda p: xfull.at[p, my_rows], lambda p: hid_p.at[p], h1_s, h1_r)
-    h2_ex = exchange(n_tp, t, tp_dev, whole(hid_p), lambda p: hid_z.at[:, p], h2_s, h2_r)
+    h1_ex = exchange(n_z, z, z_dev, lambda p: hfull.at[p, my_rows], lambda p: hid_p.at[p], h1_s, h1_r)
     c1_ex = exchange(n_z, z, z_dev, lambda p: cotfull.at[p, my_rows], lambda p: cot_p.at[p], c1_s, c1_r)
-    c2_ex = exchange(n_tp, t, tp_dev, whole(cot_p), lambda p: cot_z.at[:, p], c2_s, c2_r)
     att_ring = ring(att_z, az_s, az_r)
     gq_ring = ring(gq_z, qz_s, qz_r)
     kz_ex = exchange(n_z, z, z_dev, whole(gkv_n), lambda p: gkv_z.at[pl.ds(p * BLOCK, BLOCK)], kz_s, kz_r)
@@ -169,10 +248,10 @@
     def _():
         pl.semaphore_wait(gate, 1)
 
+    xfull[t] = x_ref[...]
     q_ex[0]()
-    x_ex[0]()
+    x_ag.start()
     sq_in[t] = sq_out[...]
-    xfull[t] = x_ref[...]
 
     def total_of(ref):
         total = ref[0]
@@ -185,26 +264,28 @@
     kv_acc[...] = jnp.zeros_like(kv_acc)
     wq_copy.wait()
 
-    @pl.loop(0, n_tp)
-    def _(i):
-        p = lax.rem(t - i + n_tp, n_tp)
-
-        @pl.when(i > 0)
-        def _():
-            x_ex[4](p).wait_recv()
-
-        gain = gain_ref[:, pl.ds(pl.multiple_of(p * part, part), part)]
-        hidden = ((xfull[p].astype(F32) * inv_b[:, :1]) * gain).astype(BF16)
-        xfull[p] = hidden
-        kv_acc[...] += mm(hidden, wq[pl.ds(pl.multiple_of(p * part, part), part), heads:])
+    def norm_block(p):
+        cols_p = pl.ds(pl.multiple_of(p * part, part), part)
+        hidden = ((xfull[p].astype(F32) * inv_b[:, :1]) * gain_ref[:, cols_p]).astype(BF16)
+        hfull[p] = hidden
+        kv_acc[...] += mm(hidden, wq[cols_p, heads:])
+
+    norm_block(t)
+    x_ag.relay()
+    for p in order[1:4]:
+        norm_block(p)
+    if n_x > 1:
+        x_ag.relay_far()
+    x_ag.finish()
 
     @pl.when(s == 1)
     def _():
         weights = jnp.broadcast_to(tw_ref[...].astype(F32), (BLOCK, BLOCK)).T[:, :1]
-        cot_loc[...] = (loss_ref[...].astype(F32) * weights).astype(BF16)
-        cotfull[t] = cot_loc[...]
-        c_ex[0]()
-        pl.semaphore_signal(gate, inc=1, device_id={"section": 1 - s}, device_id_type=MESH)
+        cotfull[t] = (loss_ref[...].astype(F32) * weights).astype(BF16)
+        c_ag.start()
+
+    for p in order[4:]:
+        norm_block(p)
 
     def project(full, weight, lo_col, n_col):
         total = jnp.zeros((BLOCK, n_col), F32)
@@ -263,26 +344,46 @@
         kv_on(0).start()
 
     for j in range(0, GROUP_HEADS, 2):
-        pair = project(xfull, wq, j * HEAD_SIZE, 2 * HEAD_SIZE)
+        pair = project(hfull, wq, j * HEAD_SIZE, 2 * HEAD_SIZE)
         q_s[j * BLOCK : (j + 1) * BLOCK] = pair[:, :HEAD_SIZE]
         q_s[(j + 1) * BLOCK : (j + 2) * BLOCK] = pair[:, HEAD_SIZE:]
     h1_ex[0]()
-    hid_p[z] = xfull[z, my_rows]
+    hid_p[z] = hfull[z, my_rows]
+
+    @pl.when(s == 1)
+    def _():
+        c_ag.relay()
+        pl.semaphore_signal(gate, inc=1, device_id={"section": 1 - s}, device_id_type=MESH)
 
     def pass_hidden():
         h1_ex[1]()
-        h2_ex[0]()
         hid_z[:, t] = hid_p[...]
+        h2_ag.start()
+
+    def relay_rest(ag):
+        if n_x > 1:
+            ag.relay_far()
+        ag.finish()
 
     def head_cotangent(arrival):
         wo_copy.wait()
         hc_acc[...] = jnp.zeros_like(hc_acc)
 
-        @pl.loop(0, n_tp)
-        def _(i):
-            p = lax.rem(t - i + n_tp, n_tp)
-            arrival(i, p)
+        def add(p):
             hc_acc[...] += mm(cotfull[p], wo[pl.ds(pl.multiple_of(p * part, part), part)])
+
+        if arrival is not None:
+            arrival()
+            add(t)
+            c_ag.relay()
+            for p in order[1:4]:
+                add(p)
+            relay_rest(c_ag)
+        else:
+            for p in order[:4]:
+                add(p)
+        for p in order[4:]:
+            add(p)
 
         for j in range(GROUP_HEADS):
             hc_s[j * BLOCK : (j + 1) * BLOCK] = hc_acc[:, j * HEAD_SIZE : (j + 1) * HEAD_SIZE].astype(BF16)
@@ -300,8 +401,8 @@
 
     @pl.when(s == 1)
     def _():
-        c_ex[1]()
-        head_cotangent(lambda i, p: None)
+        relay_rest(c_ag)
+        head_cotangent(None)
 
     doc_start = jnp.int32(0)
     doc_end = jnp.int32(0)
@@ -356,19 +457,19 @@
     for j in range(GROUP_HEADS):
         att_z[own_z, j * HEAD_SIZE : (j + 1) * HEAD_SIZE] = att_s[j * BLOCK : (j + 1) * BLOCK]
 
-    def sec_copy(p):
-        return remote(gin_ref, cotfull.at[t], sec_s.at[p], c_r.at[t], {"section": 1 - s, "tp": p})
-
-    @pl.when(s == 1)
-    def _():
-        pass_hidden()
+    def sec_copy(i):
+        return remote(gin_ref, cotfull.at[t], sec_s.at[i], c_r.at[t], {"section": 1 - s, "tp": order[i]})
+
+    targets = min(4, len(order))
 
     @pl.when(s == 0)
     def _():
+        h2_ag.relay()
         att_ring[0](1)
-
-        def arrival(i, p):
-            remote(cotfull.at[p], cotfull.at[p], sec_s.at[p], c_r.at[p], {"section": 1 - s}).wait_recv()
+        relay_rest(h2_ag)
+
+        def arrival():
+            remote(cotfull.at[t], cotfull.at[t], sec_s.at[0], c_r.at[t], {"section": 1 - s}).wait_recv()
 
         head_cotangent(arrival)
         att_ring[0](2)
@@ -411,8 +512,8 @@
 
     def pass_cot():
         c1_ex[1]()
-        c2_ex[0]()
         cot_z[:, t] = cot_p[...]
+        c2_ag.start()
 
     @pl.when(s == 0)
     def _():
@@ -445,6 +546,10 @@
     gkv_n[:, HEAD_SIZE:] = acc[BLOCK : 2 * BLOCK].astype(BF16)
     gkv_z[own_z] = gkv_n[...]
     kz_ex[0]()
+
+    @pl.when(s == 0)
+    def _():
+        c2_ag.relay()
 
     row_sum = gkv_n[:, :HEAD_SIZE].astype(F32) * kv[slot(last), :HEAD_SIZE].astype(F32)
     row_sum = row_sum + gkv_n[:, HEAD_SIZE:].astype(F32) * kv[slot(last), HEAD_SIZE:].astype(F32)
@@ -490,19 +595,18 @@
             out[:, base + k : base + k + step] = mm(turned[mine], right[:, k : k + step])
 
     def grad_of_out():
-        c2_ex[1]()
         att_ring[1]()
         turn(cot_z)
         weight_part(att_z, y_out_o, gout_ref, 0, y_copies[0])
 
     def grad_of_query():
-        h2_ex[1]()
         turn(hid_z)
         gq_ring[1]()
         weight_part(gq_z, y_out_q, gqkv_ref, 0, y_copies[1])
 
     @pl.when(s == 0)
     def _():
+        relay_rest(c2_ag)
         gq_ring[0](3)
         grad_of_out()
         gq_ring[0](4)
@@ -522,16 +626,22 @@
 
     @pl.when(s == 1)
     def _():
-        @pl.loop(0, n_tp)
-        def _(i):
-            sec_copy(lax.rem(t + i, n_tp)).start()
-
+        for i in range(targets):
+            sec_copy(i).start()
         send_cot()
-        for k in range(1, n_z // 2 + 1):
+        for k in (1, 2):
             att_ring[0](k)
             gq_ring[0](k)
-            if k == 2 or n_z == 2:
-                pass_cot()
+        pass_hidden()
+        pass_cot()
+        h2_ag.relay()
+        c2_ag.relay()
+        att_ring[0](3)
+        gq_ring[0](3)
+        relay_rest(h2_ag)
+        relay_rest(c2_ag)
+        att_ring[0](4)
+        gq_ring[0](4)
         grad_of_out()
         grad_of_query()
 
@@ -545,8 +655,11 @@
         copy.wait_recv()
         out[:, base : base + y_in.shape[1]] += y_in[...].astype(F32)
 
-    for ex in (x_ex, q_ex, f_ex, r_ex, h1_ex, h2_ex, c1_ex, c2_ex, kz_ex, att_ring, gq_ring):
+    for ex in (q_ex, f_ex, r_ex, h1_ex, c1_ex, kz_ex, att_ring, gq_ring):
         ex[2]()
+    for ag in (x_ag, h2_ag, c2_ag):
+        ag.wait_send()
+    c_ag.wait_send(3)
     for copy in y_copies:
         copy.wait_send()
 
@@ -576,11 +689,10 @@
 
     @pl.when(s == 1)
     def _():
-        c_ex[2]()
-
-        @pl.loop(0, n_tp)
-        def _(p):
-            sec_copy(p).wait_send()
+        for copy in c_ag.sends[:3]:
+            copy.wait_send()
+        for i in range(targets):
+            sec_copy(i).wait_send()
 
 
 def settle(a_in, b_in, c_in, a_out, b_out, c_out, sem):
@@ -609,7 +721,7 @@
     dma = lambda *n: pltpu.SemaphoreType.DMA(n)
     scratch = [
         vmem((width, cols)), vmem((width, heads)),
-        vmem((n_tp, BLOCK, part)), vmem((n_tp, BLOCK, part)), vmem((BLOCK, part)), vmem((BLOCK, BLOCK), F32),
+        vmem((n_tp, BLOCK, part)), vmem((n_tp, BLOCK, part)), vmem((n_tp, BLOCK, part)), vmem((BLOCK, BLOCK), F32),
         vmem((window * BLOCK, kv_cols)),
         vmem((q_rows, HEAD_SIZE)), vmem((q_rows, HEAD_SIZE)), vmem((q_rows, HEAD_SIZE)),
         vmem((BLOCK, heads)), vmem((BLOCK, kv_cols)),
@@ -625,11 +737,11 @@
         vmem((n_z * BLOCK, heads)), vmem((n_z * BLOCK, kv_cols)), vmem((part, n_z * BLOCK)),
         vmem((half, heads)), vmem((half, heads)), vmem((half, kv_cols)),
         vmem((half, heads)), vmem((half, heads)), vmem((half, kv_cols)),
-        dma(2), dma(n_tp), dma(n_tp), dma(n_tp), dma(n_tp), dma(window), dma(window), dma(1), dma(window), dma(window),
+        dma(2), dma(9), dma(n_tp + 2), dma(9), dma(n_tp + 2), dma(window), dma(window), dma(1), dma(window), dma(window),
         dma(n_tp), dma(n_tp), dma(n_tp), dma(n_tp),
-        dma(n_z), dma(n_z), dma(n_tp), dma(n_tp), dma(n_z), dma(n_z), dma(n_tp), dma(n_tp),
+        dma(n_z), dma(n_z), dma(9), dma(n_tp + 2), dma(n_z), dma(n_z), dma(9), dma(n_tp + 2),
         dma(n_z), dma(n_z), dma(n_z), dma(n_z), dma(n_z), dma(n_z),
-        dma(3), dma(3), dma(n_tp), dma(n_tp), dma(n_tp), pltpu.SemaphoreType.REGULAR,
+        dma(3), dma(3), dma(4), dma(n_tp), dma(n_tp), pltpu.SemaphoreType.REGULAR,
     ]
     in_vmem = pl.BlockSpec(memory_space=pltpu.VMEM)
     anywhere = pl.BlockSpec(memory_space=pl.ANY)

time: 129 us -> 141 us (1.093)
  Pallas kernels: 126 us -> 138 us
    pallas_call x1, Pallas kernels: 124 us -> 135 us  [body(): pl.pallas_call(functools.partial(kernel, n_ctx, n_tp, window), out_shape=...]
where the time goes in v6:
time: 141 us; the launch traced here: 138 us
  Pallas kernels  138 us (98%)
    pallas_call x1, Pallas kernels, body(): pl.pallas_call(functools.partial(kernel, n_ctx, n_tp, window), out_shape=...  135 us

profile of v6, /device:TPU:2, one launch (start us, length us, event | category | flops | bytes accessed | tf_op | source)
XLA Modules:
  0.0 138.5 jit_solution(2319740582191609535)
XLA Ops:
  0.6 135.4 %shard_map.94 = (bf16[128,512]{1,0:T(8,128)(2,1)}, f32[256,768]{1,0:T(8,128)}, f32[256,512]{1,0:T(8,128)}) custom-call(bf16[128,512]{1,0:T(8,128)(2,1)} %bitcast.9, bf16[128,512]{1,0:T(8,128)(2,1)} %bitcast.10, s32[1,128]{1,0:T(1,128)} %tw_ref.1, s32[1,3]{1,0:T(1,128)} %docs_ref.1, f32[1,4096]{1,0:T(1,128)} %gain_ref.1, bf16[4096,768]{1,0:T(8,128)(2,1)} %bitcast.7, ...), custom_call_target="tpu_custom_call" | custom-call | tf_op jit(solution)/shard_map/pallas_call | solution.py:748
  136.0 2.4 %shard_map.95 = (bf16[128,512]{1,0:T(8,128)(2,1)}, f32[256,768]{1,0:T(8,128)}, f32[256,512]{1,0:T(8,128)}) custom-call(bf16[128,512]{1,0:T(8,128)(2,1)} %get-tuple-element.9.a_in, f32[256,768]{1,0:T(8,128)} %get-tuple-element.10.b_in, f32[256,512]{1,0:T(8,128)} %get-tuple-element.11.c_in), custom_call_target="tpu_custom_call" | custom-call | tf_op jit(solution)/shard_map/pallas_call | solution.py:767

commit v7 on v3

--- a/solution.py
+++ b/solution.py
@@ -31,7 +31,7 @@
     x_ref, loss_ref, tw_ref, docs_ref, gain_ref, wq_hbm, wo_hbm,
     gin_ref, gqkv_ref, gout_ref,
     wq, wo, xfull, cotfull, cot_loc, inv_b,
-    kv, q_s, hc_s, att_s, gq_n, gkv_n, scores, probs, dscores, peak, denom, acc, row_acc,
+    kv, q_s, hc_s, att_s, gq_n, gkv_n, scores, probs, dscores, peak, denom, acc,
     dkv_part, dkv_in, feat_f, feat_out, feat_in, rs_out, rs_in,
     hid_p, cot_p, hid_z, cot_z, att_z, gq_z, gkv_z, turned,
     y_out_o, y_out_q, y_out_k, y_in_o, y_in_q, y_in_k,
@@ -168,18 +168,14 @@
     x_ex[0]()
     xfull[t] = x_ref[...]
 
+    x_ex[1]()
+
     @pl.when(s == 1)
     def _():
         weights = jnp.broadcast_to(tw_ref[...].astype(F32), (BLOCK, BLOCK)).T[:, :1]
         cot_loc[...] = (loss_ref[...].astype(F32) * weights).astype(BF16)
         cotfull[t] = cot_loc[...]
         c_ex[0]()
-
-    x_ex[1]()
-
-    @pl.when(s == 1)
-    def _():
-        pl.semaphore_signal(gate, inc=1, device_id={"section": 1 - s}, device_id_type=MESH)
 
     square = jnp.zeros((BLOCK, part), F32)
     for p in range(n_tp):
@@ -248,6 +244,10 @@
     def _():
         kv_on(0).start()
 
+    @pl.when(s == 1)
+    def _():
+        pl.semaphore_signal(gate, inc=1, device_id={"section": 1 - s}, device_id_type=MESH)
+
     for j in range(0, GROUP_HEADS, 2):
         pair = project(xfull, wq, j * HEAD_SIZE, 2 * HEAD_SIZE)
         q_s[j * BLOCK : (j + 1) * BLOCK] = pair[:, :HEAD_SIZE]
@@ -345,7 +345,7 @@
 
     @pl.when(s == 0)
     def _():
-        for k in range(1, n_z // 2 + 1):
+        for k in range(1, min(3, n_z // 2) + 1):
             att_ring[0](k)
 
         @pl.loop(0, n_tp)
@@ -353,6 +353,7 @@
             remote(cotfull.at[p], cotfull.at[p], sec_s.at[p], c_r.at[p], {"section": 1 - s}).wait_recv()
 
         head_cotangent()
+        att_ring[0](4)
 
     delta = jnp.sum(hc_s[...].astype(F32) * att_s[...].astype(F32), axis=1, keepdims=True)
 
@@ -424,24 +425,28 @@
     gkv_n[:, HEAD_SIZE:] = acc[BLOCK : 2 * BLOCK].astype(BF16)
     gkv_z[own_z] = gkv_n[...]
     kz_ex[0]()
-    row_acc[...] = jnp.zeros_like(row_acc)
+
+    row_sum = gkv_n[:, :HEAD_SIZE].astype(F32) * kv[slot(last), :HEAD_SIZE].astype(F32)
+    row_sum = row_sum + gkv_n[:, HEAD_SIZE:].astype(F32) * kv[slot(last), HEAD_SIZE:].astype(F32)
+    for j in range(GROUP_HEADS):
+        row_sum = row_sum + gq_n[:, j * HEAD_SIZE : (j + 1) * HEAD_SIZE].astype(F32) * q_s[
+            j * BLOCK : (j + 1) * BLOCK
+        ].astype(F32)
+    row_sum = jnp.sum(row_sum, axis=1, keepdims=True)
+    rs_out[...] = jnp.broadcast_to(row_sum, (BLOCK, BLOCK)).T[:8]
+    r_ex[0]()
+    rs_in[t] = rs_out[...]
 
     @pl.loop(1, n_tp + 1)
     def _(i):
         p = lax.rem(t + i, n_tp)
         total = feat_f[p] + mm(gkv_n[...], wq[pl.ds(p * part, part), heads:], NT)
-        total = total.astype(BF16)
-        feat_out[p] = total
-        row_acc[...] += total.astype(F32) * xfull[p].astype(F32)
+        feat_out[p] = total.astype(BF16)
 
         @pl.when(i < n_tp)
         def _():
             f_ex[3](p).start()
 
-    row_sum = jnp.sum(row_acc[...], axis=1, keepdims=True)
-    rs_out[...] = jnp.broadcast_to(row_sum, (BLOCK, BLOCK)).T[:8]
-    r_ex[0]()
-    rs_in[t] = rs_out[...]
     feat_in[t] = feat_out[t]
 
     y_copies = [
@@ -502,7 +507,7 @@
     def _():
         @pl.loop(0, n_tp)
         def _(i):
-            sec_copy(lax.rem(t + 1 + i, n_tp)).start()
+            sec_copy(lax.rem(t + i, n_tp)).start()
 
         send_cot()
         for k in range(1, n_z // 2 + 1):
@@ -593,7 +598,7 @@
         vmem((BLOCK, heads)), vmem((BLOCK, kv_cols)),
         vmem((window // 2, q_rows, 2 * BLOCK), F32), vmem((window // 2, q_rows, 2 * BLOCK)),
         vmem((window // 2, q_rows, 2 * BLOCK)),
-        vmem((q_rows, BLOCK), F32), vmem((q_rows, BLOCK), F32), vmem((q_rows, HEAD_SIZE), F32), vmem((BLOCK, part), F32),
+        vmem((q_rows, BLOCK), F32), vmem((q_rows, BLOCK), F32), vmem((q_rows, HEAD_SIZE), F32),
         vmem((window * BLOCK, kv_cols)), vmem((window, BLOCK, kv_cols)),
         vmem((n_tp, BLOCK, part), F32), vmem((n_tp, BLOCK, part)), vmem((n_tp, BLOCK, part)),
         vmem((8, BLOCK), F32), vmem((n_tp, 8, BLOCK), F32),

time: 126 us -> 128 us (1.016)
  the two profiles are of different devices: /device:TPU:2 before, /device:TPU:36 now
where the time goes in v7:
time: 128 us
  Pallas kernels  127 us (99%)
    pallas_call x1, Pallas kernels, body(): pl.pallas_call(functools.partial(kernel, n_ctx, n_tp, window), out_shape=...  125 us

profile of v7, /device:TPU:36, one launch (start us, length us, event | category | flops | bytes accessed | tf_op | source)
XLA Modules:
  0.0 127.7 jit_solution(6506096246251231235)
XLA Ops:
  0.6 124.6 %shard_map.94 = (bf16[128,512]{1,0:T(8,128)(2,1)}, f32[256,768]{1,0:T(8,128)}, f32[256,512]{1,0:T(8,128)}) custom-call(bf16[128,512]{1,0:T(8,128)(2,1)} %bitcast.9, bf16[128,512]{1,0:T(8,128)(2,1)} %bitcast.10, s32[1,128]{1,0:T(1,128)} %tw_ref.1, s32[1,3]{1,0:T(1,128)} %docs_ref.1, f32[1,4096]{1,0:T(1,128)} %gain_ref.1, bf16[4096,768]{1,0:T(8,128)(2,1)} %bitcast.7, ...), custom_call_target="tpu_custom_call" | custom-call | tf_op jit(solution)/shard_map/pallas_call | solution.py:618
  125.2 2.4 %shard_map.95 = (bf16[128,512]{1,0:T(8,128)(2,1)}, f32[256,768]{1,0:T(8,128)}, f32[256,512]{1,0:T(8,128)}) custom-call(bf16[128,512]{1,0:T(8,128)(2,1)} %get-tuple-element.9.a_in, f32[256,768]{1,0:T(8,128)} %get-tuple-element.10.b_in, f32[256,512]{1,0:T(8,128)} %get-tuple-element.11.c_in), custom_call_target="tpu_custom_call" | custom-call | tf_op jit(solution)/shard_map/pallas_call | solution.py:637

commit v8 on v7

--- a/solution.py
+++ b/solution.py
@@ -122,6 +122,79 @@
 
         return stage, lambda: arrive(top), wait_send
 
+    n_x = n_tp // 2
+    ty, tx = t // n_x, lax.rem(t, n_x)
+
+    def at(dy, dx):
+        return (ty if dy == 0 else 1 - ty) * n_x + lax.rem(tx + dx + n_x, n_x)
+
+    near = [at(0, -1), at(0, 1)] if n_x > 1 else []
+    mate_t = at(1, 0)
+
+    class Spread:
+        def __init__(self, piece, ss, rs):
+            self.piece, self.ss, self.rs = piece, ss, rs
+            self.sends = [self.move(t, None, 0, t, mate_t)]
+            if n_x > 1:
+                left, right = near
+                self.sends += [
+                    self.move(t, None, 1, t, right),
+                    self.move(t, None, 2, t, left),
+                    self.move(left, 0, 3, left, right),
+                    self.move(right, 1, 4, n_tp, left),
+                    self.move(mate_t, None, 5, mate_t, right),
+                    self.move(mate_t, None, 6, mate_t, left),
+                    self.move(at(1, -1), 0, 7, at(1, -1), right),
+                    self.move(at(1, 1), 1, 8, n_tp + 1, left),
+                ]
+
+        def move(self, p, side, i, r, to):
+            return remote(self.piece(p, side), self.piece(p, side), self.ss.at[i], self.rs.at[r], {"tp": to})
+
+        def arrive(self, p, side=None, r=None):
+            self.move(p, side, 0, p if r is None else r, mate_t).wait_recv()
+
+        def start(self):
+            for copy in self.sends[:3]:
+                copy.start()
+
+        def relay(self):
+            if n_x > 1:
+                for p, copy in zip(near, self.sends[3:5]):
+                    self.arrive(p)
+                    copy.start()
+            self.arrive(mate_t)
+            for copy in self.sends[5:7]:
+                copy.start()
+
+        def relay_far(self):
+            for p, copy in zip((at(1, -1), at(1, 1)), self.sends[7:]):
+                self.arrive(p)
+                copy.start()
+
+        def finish(self):
+            if n_x > 1:
+                for i, p in enumerate((at(0, 2), at(1, 2))):
+                    self.arrive(p, 0)
+                    self.arrive(p, 1, n_tp + i)
+
+        def wait_send(self):
+            for copy in self.sends:
+                copy.wait_send()
+
+        def rest(self):
+            if n_x > 1:
+                self.relay_far()
+            self.finish()
+
+    def slice_of(ref):
+        depth = n_z // 2
+
+        def piece(p, side):
+            return ref.at[:, p] if side is None else ref.at[pl.ds(side * depth, depth), p]
+
+        return piece
+
     whole = lambda ref: lambda p: ref
     share = BLOCK // n_tp
     my_rows = pl.ds(pl.multiple_of(t * share, share), share)
@@ -131,9 +204,9 @@
     f_ex = exchange(n_tp, t, tp_dev, lambda p: feat_out.at[p], lambda p: feat_in.at[p], f_s, f_r)
     r_ex = exchange(n_tp, t, tp_dev, whole(rs_out), lambda p: rs_in.at[p], r_s, r_r)
     h1_ex = exchange(n_z, z, z_dev, lambda p: xfull.at[p, my_rows], lambda p: hid_p.at[p], h1_s, h1_r)
-    h2_ex = exchange(n_tp, t, tp_dev, whole(hid_p), lambda p: hid_z.at[:, p], h2_s, h2_r)
+    h2_ag = Spread(slice_of(hid_z), h2_s, h2_r)
     c1_ex = exchange(n_z, z, z_dev, lambda p: cotfull.at[p, my_rows], lambda p: cot_p.at[p], c1_s, c1_r)
-    c2_ex = exchange(n_tp, t, tp_dev, whole(cot_p), lambda p: cot_z.at[:, p], c2_s, c2_r)
+    c2_ag = Spread(slice_of(cot_z), c2_s, c2_r)
     att_ring = ring(att_z, az_s, az_r)
     gq_ring = ring(gq_z, qz_s, qz_r)
     kz_ex = exchange(n_z, z, z_dev, whole(gkv_n), lambda p: gkv_z.at[pl.ds(p * BLOCK, BLOCK)], kz_s, kz_r)
@@ -244,9 +317,6 @@
     def _():
         kv_on(0).start()
 
-    @pl.when(s == 1)
-    def _():
-        pl.semaphore_signal(gate, inc=1, device_id={"section": 1 - s}, device_id_type=MESH)
 
     for j in range(0, GROUP_HEADS, 2):
         pair = project(xfull, wq, j * HEAD_SIZE, 2 * HEAD_SIZE)
@@ -257,8 +327,8 @@
 
     def pass_hidden():
         h1_ex[1]()
-        h2_ex[0]()
         hid_z[:, t] = hid_p[...]
+        h2_ag.start()
 
     def head_cotangent():
         wo_copy.wait()
@@ -281,6 +351,7 @@
     @pl.when(s == 1)
     def _():
         c_ex[1]()
+        pl.semaphore_signal(gate, inc=1, device_id={"section": 1 - s}, device_id_type=MESH)
         head_cotangent()
 
     doc_start = jnp.int32(0)
@@ -345,15 +416,16 @@
 
     @pl.when(s == 0)
     def _():
-        for k in range(1, min(3, n_z // 2) + 1):
-            att_ring[0](k)
+        h2_ag.relay()
+        att_ring[0](1)
+        h2_ag.rest()
 
         @pl.loop(0, n_tp)
         def _(p):
             remote(cotfull.at[p], cotfull.at[p], sec_s.at[p], c_r.at[p], {"section": 1 - s}).wait_recv()
 
         head_cotangent()
-        att_ring[0](4)
+        att_ring[0](2)
 
     delta = jnp.sum(hc_s[...].astype(F32) * att_s[...].astype(F32), axis=1, keepdims=True)
 
@@ -393,13 +465,18 @@
 
     def pass_cot():
         c1_ex[1]()
-        c2_ex[0]()
         cot_z[:, t] = cot_p[...]
+        c2_ag.start()
 
     @pl.when(s == 0)
     def _():
         send_cot()
         gq_ring[0](1)
+        att_ring[0](3)
+
+    @pl.when(s == 1)
+    def _():
+        h2_ag.relay()
 
     @pl.loop(0, n_tp)
     def _(p):
@@ -409,6 +486,9 @@
     def _():
         pass_cot()
         gq_ring[0](2)
+        att_ring[0](4)
+        c2_ag.relay()
+        c2_ag.rest()
 
     acc[:BLOCK] = dkv_part[slot(last), :HEAD_SIZE].astype(F32)
     acc[BLOCK : 2 * BLOCK] = dkv_part[slot(last), HEAD_SIZE:].astype(F32)
@@ -470,13 +550,11 @@
             out[:, base + k : base + k + step] = mm(turned[mine], right[:, k : k + step])
 
     def grad_of_out():
-        c2_ex[1]()
         att_ring[1]()
         turn(cot_z)
         weight_part(att_z, y_out_o, gout_ref, 0, y_copies[0])
 
     def grad_of_query():
-        h2_ex[1]()
         turn(hid_z)
         gq_ring[1]()
         weight_part(gq_z, y_out_q, gqkv_ref, 0, y_copies[1])
@@ -510,11 +588,17 @@
             sec_copy(lax.rem(t + i, n_tp)).start()
 
         send_cot()
-        for k in range(1, n_z // 2 + 1):
+        for k in (1, 2):
             att_ring[0](k)
             gq_ring[0](k)
-            if k == 2 or n_z == 2:
-                pass_cot()
+        h2_ag.rest()
+        pass_cot()
+        att_ring[0](3)
+        gq_ring[0](3)
+        c2_ag.relay()
+        att_ring[0](4)
+        gq_ring[0](4)
+        c2_ag.rest()
         grad_of_out()
         grad_of_query()
 
@@ -528,8 +612,10 @@
         copy.wait_recv()
         out[:, base : base + y_in.shape[1]] += y_in[...].astype(F32)
 
-    for ex in (x_ex, f_ex, r_ex, h1_ex, h2_ex, c1_ex, c2_ex, kz_ex, att_ring, gq_ring):
+    for ex in (x_ex, f_ex, r_ex, h1_ex, c1_ex, kz_ex, att_ring, gq_ring):
         ex[2]()
+    for ag in (h2_ag, c2_ag):
+        ag.wait_send()
     for copy in y_copies:
         copy.wait_send()
 
@@ -609,7 +695,7 @@
         vmem((half, heads)), vmem((half, heads)), vmem((half, kv_cols)),
         dma(2), dma(n_tp), dma(n_tp), dma(n_tp), dma(n_tp), dma(window), dma(window), dma(1), dma(window), dma(window),
         dma(n_tp), dma(n_tp), dma(n_tp), dma(n_tp),
-        dma(n_z), dma(n_z), dma(n_tp), dma(n_tp), dma(n_z), dma(n_z), dma(n_tp), dma(n_tp),
+        dma(n_z), dma(n_z), dma(9), dma(n_tp + 2), dma(n_z), dma(n_z), dma(9), dma(n_tp + 2),
         dma(n_z), dma(n_z), dma(n_z), dma(n_z), dma(n_z), dma(n_z),
         dma(3), dma(3), dma(n_tp), pltpu.SemaphoreType.REGULAR,
     ]

time: 128 us -> 139 us (1.086)
  the two profiles are of different devices: /device:TPU:36 before, /device:TPU:2 now
where the time goes in v8:
time: 139 us
  Pallas kernels  139 us (100%)
    pallas_call x1, Pallas kernels, body(): pl.pallas_call(functools.partial(kernel, n_ctx, n_tp, window), out_shape=...  136 us

profile of v8, /device:TPU:2, one launch (start us, length us, event | category | flops | bytes accessed | tf_op | source)
XLA Modules:
  0.0 139.3 jit_solution(9725521229785000328)
XLA Ops:
  0.6 136.3 %shard_map.94 = (bf16[128,512]{1,0:T(8,128)(2,1)}, f32[256,768]{1,0:T(8,128)}, f32[256,512]{1,0:T(8,128)}) custom-call(bf16[128,512]{1,0:T(8,128)(2,1)} %bitcast.9, bf16[128,512]{1,0:T(8,128)(2,1)} %bitcast.10, s32[1,128]{1,0:T(1,128)} %tw_ref.1, s32[1,3]{1,0:T(1,128)} %docs_ref.1, f32[1,4096]{1,0:T(1,128)} %gain_ref.1, bf16[4096,768]{1,0:T(8,128)(2,1)} %bitcast.7, ...), custom_call_target="tpu_custom_call" | custom-call | tf_op jit(solution)/shard_map/pallas_call | solution.py:704
  136.9 2.4 %shard_map.95 = (bf16[128,512]{1,0:T(8,128)(2,1)}, f32[256,768]{1,0:T(8,128)}, f32[256,512]{1,0:T(8,128)}) custom-call(bf16[128,512]{1,0:T(8,128)(2,1)} %get-tuple-element.9.a_in, f32[256,768]{1,0:T(8,128)} %get-tuple-element.10.b_in, f32[256,512]{1,0:T(8,128)} %get-tuple-element.11.c_in), custom_call_target="tpu_custom_call" | custom-call | tf_op jit(solution)/shard_map/pallas_call | solution.py:723

commit v9 on v7

--- a/solution.py
+++ b/solution.py
@@ -172,10 +172,7 @@
 
     @pl.when(s == 1)
     def _():
-        weights = jnp.broadcast_to(tw_ref[...].astype(F32), (BLOCK, BLOCK)).T[:, :1]
-        cot_loc[...] = (loss_ref[...].astype(F32) * weights).astype(BF16)
-        cotfull[t] = cot_loc[...]
-        c_ex[0]()
+        pl.semaphore_signal(gate, inc=1, device_id={"section": 1 - s}, device_id_type=MESH)
 
     square = jnp.zeros((BLOCK, part), F32)
     for p in range(n_tp):
@@ -244,10 +241,6 @@
     def _():
         kv_on(0).start()
 
-    @pl.when(s == 1)
-    def _():
-        pl.semaphore_signal(gate, inc=1, device_id={"section": 1 - s}, device_id_type=MESH)
-
     for j in range(0, GROUP_HEADS, 2):
         pair = project(xfull, wq, j * HEAD_SIZE, 2 * HEAD_SIZE)
         q_s[j * BLOCK : (j + 1) * BLOCK] = pair[:, :HEAD_SIZE]
@@ -267,6 +260,13 @@
             hc_s[j * BLOCK : (j + 1) * BLOCK] = pair[:, :HEAD_SIZE]
             hc_s[(j + 1) * BLOCK : (j + 2) * BLOCK] = pair[:, HEAD_SIZE:]
 
+    @pl.when(s == 1)
+    def _():
+        weights = jnp.broadcast_to(tw_ref[...].astype(F32), (BLOCK, BLOCK)).T[:, :1]
+        cot_loc[...] = (loss_ref[...].astype(F32) * weights).astype(BF16)
+        cotfull[t] = cot_loc[...]
+        c_ex[0]()
+
     @pl.loop(1, steps_z)
     def _(k):
         @pl.when(z - k >= 0)
@@ -277,11 +277,6 @@
     @pl.when(s == 0)
     def _():
         pass_hidden()
-
-    @pl.when(s == 1)
-    def _():
-        c_ex[1]()
-        head_cotangent()
 
     doc_start = jnp.int32(0)
     doc_end = jnp.int32(0)
@@ -341,7 +336,8 @@
 
     @pl.when(s == 1)
     def _():
-        pass_hidden()
+        c_ex[1]()
+        head_cotangent()
 
     @pl.when(s == 0)
     def _():
@@ -400,6 +396,10 @@
     def _():
         send_cot()
         gq_ring[0](1)
+
+    @pl.when(s == 1)
+    def _():
+        pass_hidden()
 
     @pl.loop(0, n_tp)
     def _(p):
@@ -513,8 +513,7 @@
         for k in range(1, n_z // 2 + 1):
             att_ring[0](k)
             gq_ring[0](k)
-            if k == 2 or n_z == 2:
-                pass_cot()
+        pass_cot()
         grad_of_out()
         grad_of_query()
 

time: 128 us -> 133 us (1.039)
  the two profiles are of different devices: /device:TPU:36 before, /device:TPU:2 now
where the time goes in v9:
time: 133 us; the launch traced here: 130 us
  Pallas kernels  130 us (98%)
    pallas_call x1, Pallas kernels, body(): pl.pallas_call(functools.partial(kernel, n_ctx, n_tp, window), out_shape=...  127 us

profile of v9, /device:TPU:2, one launch (start us, length us, event | category | flops | bytes accessed | tf_op | source)
XLA Modules:
  0.0 130.2 jit_solution(12039316631226801527)
XLA Ops:
  0.6 127.1 %shard_map.94 = (bf16[128,512]{1,0:T(8,128)(2,1)}, f32[256,768]{1,0:T(8,128)}, f32[256,512]{1,0:T(8,128)}) custom-call(bf16[128,512]{1,0:T(8,128)(2,1)} %bitcast.9, bf16[128,512]{1,0:T(8,128)(2,1)} %bitcast.10, s32[1,128]{1,0:T(1,128)} %tw_ref.1, s32[1,3]{1,0:T(1,128)} %docs_ref.1, f32[1,4096]{1,0:T(1,128)} %gain_ref.1, bf16[4096,768]{1,0:T(8,128)(2,1)} %bitcast.7, ...), custom_call_target="tpu_custom_call" | custom-call | tf_op jit(solution)/shard_map/pallas_call | solution.py:617
  127.8 2.4 %shard_map.95 = (bf16[128,512]{1,0:T(8,128)(2,1)}, f32[256,768]{1,0:T(8,128)}, f32[256,512]{1,0:T(8,128)}) custom-call(bf16[128,512]{1,0:T(8,128)(2,1)} %get-tuple-element.9.a_in, f32[256,768]{1,0:T(8,128)} %get-tuple-element.10.b_in, f32[256,512]{1,0:T(8,128)} %get-tuple-element.11.c_in), custom_call_target="tpu_custom_call" | custom-call | tf_op jit(solution)/shard_map/pallas_call | solution.py:636

commit v10 on v7

--- a/solution.py
+++ b/solution.py
@@ -278,11 +278,6 @@
     def _():
         pass_hidden()
 
-    @pl.when(s == 1)
-    def _():
-        c_ex[1]()
-        head_cotangent()
-
     doc_start = jnp.int32(0)
     doc_end = jnp.int32(0)
     for i in range(docs_ref.shape[1]):
@@ -341,11 +336,13 @@
 
     @pl.when(s == 1)
     def _():
+        c_ex[1]()
+        head_cotangent()
         pass_hidden()
 
     @pl.when(s == 0)
     def _():
-        for k in range(1, min(3, n_z // 2) + 1):
+        for k in (1, 2):
             att_ring[0](k)
 
         @pl.loop(0, n_tp)
@@ -353,7 +350,7 @@
             remote(cotfull.at[p], cotfull.at[p], sec_s.at[p], c_r.at[p], {"section": 1 - s}).wait_recv()
 
         head_cotangent()
-        att_ring[0](4)
+        att_ring[0](3)
 
     delta = jnp.sum(hc_s[...].astype(F32) * att_s[...].astype(F32), axis=1, keepdims=True)
 
@@ -400,6 +397,7 @@
     def _():
         send_cot()
         gq_ring[0](1)
+        att_ring[0](4)
 
     @pl.loop(0, n_tp)
     def _(p):
@@ -513,8 +511,7 @@
         for k in range(1, n_z // 2 + 1):
             att_ring[0](k)
             gq_ring[0](k)
-            if k == 2 or n_z == 2:
-                pass_cot()
+        pass_cot()
         grad_of_out()
         grad_of_query()
 

time: 128 us -> 129 us (level)
  the two profiles are of different devices: /device:TPU:36 before, /device:TPU:2 now
where the time goes in v10:
time: 129 us
  Pallas kernels  129 us (100%)
    pallas_call x1, Pallas kernels, body(): pl.pallas_call(functools.partial(kernel, n_ctx, n_tp, window), out_shape=...  126 us

profile of v10, /device:TPU:2, one launch (start us, length us, event | category | flops | bytes accessed | tf_op | source)
XLA Modules:
  0.0 129.1 jit_solution(4405745087855322414)
XLA Ops:
  0.6 126.1 %shard_map.94 = (bf16[128,512]{1,0:T(8,128)(2,1)}, f32[256,768]{1,0:T(8,128)}, f32[256,512]{1,0:T(8,128)}) custom-call(bf16[128,512]{1,0:T(8,128)(2,1)} %bitcast.9, bf16[128,512]{1,0:T(8,128)(2,1)} %bitcast.10, s32[1,128]{1,0:T(1,128)} %tw_ref.1, s32[1,3]{1,0:T(1,128)} %docs_ref.1, f32[1,4096]{1,0:T(1,128)} %gain_ref.1, bf16[4096,768]{1,0:T(8,128)(2,1)} %bitcast.7, ...), custom_call_target="tpu_custom_call" | custom-call | tf_op jit(solution)/shard_map/pallas_call | solution.py:615
  126.7 2.4 %shard_map.95 = (bf16[128,512]{1,0:T(8,128)(2,1)}, f32[256,768]{1,0:T(8,128)}, f32[256,512]{1,0:T(8,128)}) custom-call(bf16[128,512]{1,0:T(8,128)(2,1)} %get-tuple-element.9.a_in, f32[256,768]{1,0:T(8,128)} %get-tuple-element.10.b_in, f32[256,512]{1,0:T(8,128)} %get-tuple-element.11.c_in), custom_call_target="tpu_custom_call" | custom-call | tf_op jit(solution)/shard_map/pallas_call | solution.py:634

commit v11 on v3

--- a/solution.py
+++ b/solution.py
@@ -32,11 +32,11 @@
     gin_ref, gqkv_ref, gout_ref,
     wq, wo, xfull, cotfull, cot_loc, inv_b,
     kv, q_s, hc_s, att_s, gq_n, gkv_n, scores, probs, dscores, peak, denom, acc, row_acc,
-    dkv_part, dkv_in, feat_f, feat_out, feat_in, rs_out, rs_in,
+    dkv_part, dkv_in, dkv_mate, dkv_sum, feat_f, feat_out, feat_in, rs_out, rs_in,
     hid_p, cot_p, hid_z, cot_z, att_z, gq_z, gkv_z, turned,
     y_out_o, y_out_q, y_out_k, y_in_o, y_in_q, y_in_k,
     w_sem, x_s, x_r, c_s, c_r, kv_s, kv_r, kv_f, d_s, d_r, f_s, f_r, r_s, r_r,
-    h1_s, h1_r, h2_s, h2_r, c1_s, c1_r, c2_s, c2_r, az_s, az_r, qz_s, qz_r, kz_s, kz_r, y_s, y_r, sec_s, gate,
+    h1_s, h1_r, h2_s, h2_r, c1_s, c1_r, c2_s, c2_r, az_s, az_r, qz_s, qz_r, kz_s, kz_r, y_s, y_r, sec_s, m_s, m_r, gate,
 ):
     s = lax.axis_index("section")
     c = lax.axis_index("ctx")
@@ -356,11 +356,50 @@
 
     delta = jnp.sum(hc_s[...].astype(F32) * att_s[...].astype(F32), axis=1, keepdims=True)
 
-    def dkv_copy(d):
+    def dkv_mate_copy(d, k):
+        return remote(dkv_part.at[slot(last - d)], dkv_mate.at[k], m_s.at[k], m_r.at[k], mate)
+
+    def dkv_next():
+        return remote(dkv_part.at[slot(last - 1)], dkv_in.at[0], d_s.at[0], d_r.at[0], mate)
+
+    def dkv_far():
         return remote(
-            dkv_part.at[slot(last - d)], dkv_in.at[d], d_s.at[d], d_r.at[d],
-            {"ctx": lax.rem(c - d + n_ctx, n_ctx)},
+            dkv_part.at[slot(0)], dkv_in.at[steps_z], d_s.at[steps_z], d_r.at[steps_z],
+            {"ctx": lax.rem(c - far + n_ctx, n_ctx)},
         )
+
+    def dkv_down(k):
+        return remote(
+            dkv_sum.at[k], dkv_in.at[k], d_s.at[k], d_r.at[k], {"ctx": lax.rem(c - 2 * k + n_ctx, n_ctx)}
+        )
+
+    def dkv_send_mate(d):
+        for side in (0, 1):
+            k = (d + 1) // 2 - side
+
+            @pl.when(lo == side)
+            def _():
+                if k == steps_z:
+
+                    @pl.when(c - far >= 0)
+                    def _():
+                        dkv_far().start()
+
+                elif k == 0:
+                    dkv_next().start()
+                else:
+
+                    @pl.when(z - k >= 0)
+                    def _():
+                        dkv_mate_copy(d, k).start()
+
+    def dkv_add(k):
+        @pl.when(z - k >= 0)
+        def _():
+            dkv_mate_copy(1, k).wait_recv()
+            own_part = dkv_part[slot(last - 2 * k)].astype(F32)
+            dkv_sum[k] = (own_part + dkv_mate[k].astype(F32)).astype(BF16)
+            dkv_down(k).start()
 
     for g in range(pairs):
         block = slice(g * 2 * BLOCK, (g + 1) * 2 * BLOCK)
@@ -369,13 +408,11 @@
         dkv_part[block, :HEAD_SIZE] = (mm(ds, q_s[...], TN) * scale).astype(BF16)
         dkv_part[block, HEAD_SIZE:] = mm(probs[g], hc_s[...], TN).astype(BF16)
         dscores[g] = ds
-        for j in (2 * g, 2 * g + 1):
-            if j < last:
-
-                @pl.when(c - last + j >= 0)
-                def _():
-                    dkv_copy(last - j).start()
-
+        dkv_send_mate(last - 2 * g)
+        if g >= 2:
+            dkv_add(pairs + 1 - g)
+
+    dkv_add(1)
     total = mm(dscores[0], keys(0))
     for g in range(1, pairs):
         total = total + mm(dscores[g], keys(g))
@@ -412,13 +449,24 @@
     acc[:BLOCK] = dkv_part[slot(last), :HEAD_SIZE].astype(F32)
     acc[BLOCK : 2 * BLOCK] = dkv_part[slot(last), HEAD_SIZE:].astype(F32)
 
-    @pl.loop(1, window)
-    def _(d):
-        @pl.when(c + d < n_ctx)
+    def dkv_take(copy, k):
+        copy.wait_recv()
+        acc[:BLOCK] += dkv_in[k, :, :HEAD_SIZE].astype(F32)
+        acc[BLOCK : 2 * BLOCK] += dkv_in[k, :, HEAD_SIZE:].astype(F32)
+
+    @pl.when(lo == 0)
+    def _():
+        dkv_take(dkv_next(), 0)
+
+    @pl.loop(1, steps_z)
+    def _(k):
+        @pl.when(z + k < n_z)
         def _():
-            dkv_copy(d).wait_recv()
-            acc[:BLOCK] += dkv_in[d, :, :HEAD_SIZE].astype(F32)
-            acc[BLOCK : 2 * BLOCK] += dkv_in[d, :, HEAD_SIZE:].astype(F32)
+            dkv_take(dkv_down(k), k)
+
+    @pl.when((lo == 1) & (c + far < n_ctx))
+    def _():
+        dkv_take(dkv_far(), steps_z)
 
     gkv_n[:, :HEAD_SIZE] = acc[:BLOCK].astype(BF16)
     gkv_n[:, HEAD_SIZE:] = acc[BLOCK : 2 * BLOCK].astype(BF16)
@@ -546,11 +594,20 @@
     def _():
         kv_on(0).wait_send()
 
-    @pl.loop(1, window)
-    def _(d):
-        @pl.when(c - d >= 0)
+    @pl.loop(1, steps_z)
+    def _(k):
+        @pl.when(z - k >= 0)
         def _():
-            dkv_copy(d).wait_send()
+            dkv_mate_copy(1, k).wait_send()
+            dkv_down(k).wait_send()
+
+    @pl.when(lo == 1)
+    def _():
+        dkv_next().wait_send()
+
+    @pl.when((lo == 0) & (c - far >= 0))
+    def _():
+        dkv_far().wait_send()
 
     @pl.when(s == 1)
     def _():
@@ -595,6 +652,7 @@
         vmem((window // 2, q_rows, 2 * BLOCK)),
         vmem((q_rows, BLOCK), F32), vmem((q_rows, BLOCK), F32), vmem((q_rows, HEAD_SIZE), F32), vmem((BLOCK, part), F32),
         vmem((window * BLOCK, kv_cols)), vmem((window, BLOCK, kv_cols)),
+        vmem((window // 2, BLOCK, kv_cols)), vmem((window // 2, BLOCK, kv_cols)),
         vmem((n_tp, BLOCK, part), F32), vmem((n_tp, BLOCK, part)), vmem((n_tp, BLOCK, part)),
         vmem((8, BLOCK), F32), vmem((n_tp, 8, BLOCK), F32),
         vmem((n_z, share, part)), vmem((n_z, share, part)),
@@ -606,7 +664,7 @@
         dma(n_tp), dma(n_tp), dma(n_tp), dma(n_tp),
         dma(n_z), dma(n_z), dma(n_tp), dma(n_tp), dma(n_z), dma(n_z), dma(n_tp), dma(n_tp),
         dma(n_z), dma(n_z), dma(n_z), dma(n_z), dma(n_z), dma(n_z),
-        dma(3), dma(3), dma(n_tp), pltpu.SemaphoreType.REGULAR,
+        dma(3), dma(3), dma(n_tp), dma(window), dma(window), pltpu.SemaphoreType.REGULAR,
     ]
     in_vmem = pl.BlockSpec(memory_space=pltpu.VMEM)
     anywhere = pl.BlockSpec(memory_space=pl.ANY)

time: 126 us -> 126 us (level)
  no operation moved by 1% of the time
where the time goes in v11:
time: 126 us; the launch traced here: 125 us
  Pallas kernels  124 us (98%)
    pallas_call x1, Pallas kernels, body(): pl.pallas_call(functools.partial(kernel, n_ctx, n_tp, window), out_shape=...  122 us

profile of v11, /device:TPU:2, one launch (start us, length us, event | category | flops | bytes accessed | tf_op | source)
XLA Modules:
  0.0 125.0 jit_solution(6862172529920443120)
XLA Ops:
  0.6 121.9 %shard_map.94 = (bf16[128,512]{1,0:T(8,128)(2,1)}, f32[256,768]{1,0:T(8,128)}, f32[256,512]{1,0:T(8,128)}) custom-call(bf16[128,512]{1,0:T(8,128)(2,1)} %bitcast.9, bf16[128,512]{1,0:T(8,128)(2,1)} %bitcast.10, s32[1,128]{1,0:T(1,128)} %tw_ref.1, s32[1,3]{1,0:T(1,128)} %docs_ref.1, f32[1,4096]{1,0:T(1,128)} %gain_ref.1, bf16[4096,768]{1,0:T(8,128)(2,1)} %bitcast.7, ...), custom_call_target="tpu_custom_call" | custom-call | tf_op jit(solution)/shard_map/pallas_call | solution.py:671
  122.6 2.4 %shard_map.95 = (bf16[128,512]{1,0:T(8,128)(2,1)}, f32[256,768]{1,0:T(8,128)}, f32[256,512]{1,0:T(8,128)}) custom-call(bf16[128,512]{1,0:T(8,128)(2,1)} %get-tuple-element.9.a_in, f32[256,768]{1,0:T(8,128)} %get-tuple-element.10.b_in, f32[256,512]{1,0:T(8,128)} %get-tuple-element.11.c_in), custom_call_target="tpu_custom_call" | custom-call | tf_op jit(solution)/shard_map/pallas_call | solution.py:690

commit v12 on v11

--- a/solution.py
+++ b/solution.py
@@ -345,14 +345,14 @@
 
     @pl.when(s == 0)
     def _():
-        for k in range(1, n_z // 2 + 1):
-            att_ring[0](k)
+        att_ring[0](1)
 
         @pl.loop(0, n_tp)
         def _(p):
             remote(cotfull.at[p], cotfull.at[p], sec_s.at[p], c_r.at[p], {"section": 1 - s}).wait_recv()
 
         head_cotangent()
+        att_ring[0](2)
 
     delta = jnp.sum(hc_s[...].astype(F32) * att_s[...].astype(F32), axis=1, keepdims=True)
 
@@ -436,6 +436,7 @@
     def _():
         send_cot()
         gq_ring[0](1)
+        att_ring[0](3)
 
     @pl.loop(0, n_tp)
     def _(p):
@@ -445,6 +446,7 @@
     def _():
         pass_cot()
         gq_ring[0](2)
+        att_ring[0](4)
 
     acc[:BLOCK] = dkv_part[slot(last), :HEAD_SIZE].astype(F32)
     acc[BLOCK : 2 * BLOCK] = dkv_part[slot(last), HEAD_SIZE:].astype(F32)

time: 126 us -> 127 us (level)
  no operation moved by 1% of the time
where the time goes in v12:
time: 127 us; the launch traced here: 125 us
  Pallas kernels  125 us (98%)
    pallas_call x1, Pallas kernels, body(): pl.pallas_call(functools.partial(kernel, n_ctx, n_tp, window), out_shape=...  122 us

profile of v12, /device:TPU:2, one launch (start us, length us, event | category | flops | bytes accessed | tf_op | source)
XLA Modules:
  0.0 125.1 jit_solution(14789949627984937271)
XLA Ops:
  0.6 122.1 %shard_map.94 = (bf16[128,512]{1,0:T(8,128)(2,1)}, f32[256,768]{1,0:T(8,128)}, f32[256,512]{1,0:T(8,128)}) custom-call(bf16[128,512]{1,0:T(8,128)(2,1)} %bitcast.9, bf16[128,512]{1,0:T(8,128)(2,1)} %bitcast.10, s32[1,128]{1,0:T(1,128)} %tw_ref.1, s32[1,3]{1,0:T(1,128)} %docs_ref.1, f32[1,4096]{1,0:T(1,128)} %gain_ref.1, bf16[4096,768]{1,0:T(8,128)(2,1)} %bitcast.7, ...), custom_call_target="tpu_custom_call" | custom-call | tf_op jit(solution)/shard_map/pallas_call | solution.py:673
  122.7 2.4 %shard_map.95 = (bf16[128,512]{1,0:T(8,128)(2,1)}, f32[256,768]{1,0:T(8,128)}, f32[256,512]{1,0:T(8,128)}) custom-call(bf16[128,512]{1,0:T(8,128)(2,1)} %get-tuple-element.9.a_in, f32[256,768]{1,0:T(8,128)} %get-tuple-element.10.b_in, f32[256,512]{1,0:T(8,128)} %get-tuple-element.11.c_in), custom_call_target="tpu_custom_call" | custom-call | tf_op jit(solution)/shard_map/pallas_call | solution.py:692
